TPU v7x, 256 devices: a whole 4x4x8 slice. The times are simulated.
256 devices in a mesh: tm: 2 (over core), space: 32 (over z, x), dp: 4 (over y).
Axes of the slice: x: 4, y: 4, z: 8, core: 2. Of those that a mesh axis runs over, the one named last changes fastest.
Arguments:
- features: bfloat16 [4, 6, 64, 104, 384], P('dp', 'tm', 'space'), may hold values from -6 to 6
- frame_index: int32 [4, 6], P('dp', 'tm'), may hold values from 0 to 15, as said below
- conv_weight: bfloat16 [10368, 384], P('dp'), may hold values from -0.0625 to 0.0625
- conv_bias: float32 [384], replicated, may hold values from -3 to 3
- norm_gain: float32 [384], replicated, may hold values from 0.25 to 1.75
- attn_gain: float32 [384], replicated, may hold values from 0.25 to 1.75
- qkv_weight: bfloat16 [384, 1152], P('dp'), may hold values from -2 to 2
- out_weight: bfloat16 [384, 384], P('dp'), may hold values from -0.3125 to 0.3125
Outputs:
- decoded: bfloat16 [4, 6, 64, 104, 384], P('dp', 'tm', 'space')
Inputs may be any that keep to these rules, and one draw needn't show every extreme that they name: Along f, frame_index rises by one within a video and restarts at 0 where a new video begins; every video spans 9 to 16 frames, of which the slots may hold only a tail or a head.
All inputs are finite; a program needn't handle non-finite values.
Results may differ from a plain program's by a relative error of at most 0.029.
Values may be sent and summed in bfloat16 or wider, within the bound.
A program may use at most 192 MiB of HBM per device.

v0:
```python
import jax
import jax.numpy as jnp
from jax import lax
from jax.sharding import PartitionSpec as P

EPS = 1e-06


def with_halo(cells, sides, width):
    for axis, dim in sides:
        count = lax.axis_size(axis)
        ends = count - 1
        head = lax.slice_in_dim(cells, 0, width, axis=dim)
        tail = lax.slice_in_dim(cells, cells.shape[dim] - width, cells.shape[dim], axis=dim)
        cells = jnp.concatenate(
            [
                lax.ppermute(tail, axis, [(i, (i + 1) % count) for i in range(ends)]),
                cells,
                lax.ppermute(head, axis, [((i + 1) % count, i) for i in range(ends)]),
            ],
            axis=dim,
        )
    return cells


def passed_along(value, axis, steps):
    count = lax.axis_size(axis)
    first, last = (max(0, -steps), min(count, count - steps))
    return lax.ppermute(value, axis, [(source, source + steps) for source in range(first, last)])


def rms_scale(values, gain):
    values = values.astype(jnp.float32)
    return values * lax.rsqrt(jnp.mean(values * values, axis=-1, keepdims=True) + EPS) * gain


def build_patches(sources, rows, width):
    windows = []
    for source in sources:
        for tap_h in range(3):
            for tap_w in range(3):
                windows.append(source[:, tap_h : tap_h + rows, tap_w : tap_w + width, :])
    joined = jnp.concatenate(windows, axis=-1)
    return joined.reshape(-1, joined.shape[-1])


def on_device(
    features, frame_index, conv_weight, conv_bias, norm_gain, attn_gain, qkv_weight, out_weight
):
    frames, rows, width, chans = (
        features.shape[1],
        features.shape[2],
        features.shape[3],
        features.shape[4],
    )
    pixels = rows * width
    full_qkv, full_out = (
        lax.all_gather(qkv_weight, "dp", axis=0, tiled=True),
        lax.all_gather(out_weight, "dp", axis=0, tiled=True),
    )
    local = features[0]
    activated = jax.nn.silu(rms_scale(local, norm_gain)).astype(jnp.bfloat16)
    rimmed = with_halo(activated, (("space", 1),), 1)
    rimmed = jnp.pad(rimmed, ((0, 0), (0, 0), (1, 1), (0, 0)))
    prior = passed_along(rimmed[frames - 2 :], "tm", 1)
    sequence = jnp.concatenate([prior, rimmed], axis=0)
    position = frame_index[0]
    keep_one = (position >= 1).astype(jnp.bfloat16)[:, None, None, None]
    keep_two = (position >= 2).astype(jnp.bfloat16)[:, None, None, None]
    earlier = sequence[1 : frames + 1] * keep_one
    oldest = sequence[:frames] * keep_two
    patches = build_patches((oldest, earlier, rimmed), rows, width)
    conv = jnp.dot(
        patches,
        lax.all_gather(conv_weight, "dp", axis=0, tiled=True),
        preferred_element_type=jnp.float32,
    )
    hidden = (local.reshape(frames * pixels, chans).astype(jnp.float32) + conv + conv_bias).astype(
        jnp.bfloat16
    )
    normed = rms_scale(hidden, attn_gain).astype(jnp.bfloat16)
    query = jnp.dot(normed, full_qkv[:, :chans], preferred_element_type=jnp.float32).astype(
        jnp.bfloat16
    )
    query = query.reshape(frames, pixels, chans)
    key_value_weight = full_qkv[:, chans:]
    local_pairs = jnp.dot(normed, key_value_weight, preferred_element_type=jnp.float32).astype(
        jnp.bfloat16
    )
    local_pairs = local_pairs.reshape(frames, pixels, 2 * chans)
    frame_pairs = lax.all_gather(local_pairs, "space", axis=1, tiled=True)
    keys = frame_pairs[:, :, :chans]
    values = frame_pairs[:, :, chans:]
    scale = 1.0 / jnp.sqrt(jnp.float32(chans))
    scores = jnp.einsum("fqc,fkc->fqk", query, keys, preferred_element_type=jnp.float32) * scale
    shifted = jnp.exp(scores - jnp.max(scores, axis=-1, keepdims=True))
    probs = (shifted / jnp.sum(shifted, axis=-1, keepdims=True)).astype(jnp.bfloat16)
    attended = jnp.einsum("fqk,fkc->fqc", probs, values, preferred_element_type=jnp.float32).astype(
        jnp.bfloat16
    )
    attended = attended.reshape(frames * pixels, chans)
    result = hidden.astype(jnp.float32) + jnp.dot(
        attended, full_out, preferred_element_type=jnp.float32
    )
    return result.astype(jnp.bfloat16).reshape(1, frames, rows, width, chans)


def solution(mesh):
    placed = (
        P("dp", "tm", "space", None, None),
        P("dp", "tm"),
        P("dp", None),
        P(),
        P(),
        P(),
        P("dp", None),
        P("dp", None),
    )
    return jax.shard_map(
        on_device,
        mesh=mesh,
        in_specs=placed,
        out_specs=P("dp", "tm", "space", None, None),
        check_vma=False,
    )
```

profile of v0, /device:TPU:1, one launch (start us, length us, event | category | flops | bytes accessed | tf_op | source)
XLA Modules:
  0.0 386.2 jit_solution(9901102617551294107)
XLA Ops:
  7.3 1.2 fusion.27
  8.5 1.4 multiply_convert_fusion
  10.0 4.0 %collective-permute-start = (bf16[3,1,104,384]{3,2,1,0:T(8,128)(2,1)S(1)}, bf16[3,1,104,384]{3,2,1,0:T(8,128)(2,1)S(1)}, u32[]{:S(2)}, u32[]{:S(2)}) collective-permute-start(bf16[3,1,104,384]{3,2,1,0:T(8,128)(2,1)S(1)} %get-tuple-element.7), channel_id=1, source_target_pairs={{0,4},{4,8},{8,12},{12,16},{16,20},{20,24},{24,28},{28,32},{32,36}... | collective-permute-start | bytes 718856 | tf_op jit(solution)/shard_map/ppermute | solution.py:17
  14.0 1.3 collective-permute-start.1
  15.3 3.2 collective-permute-done
  18.4 3.8 collective-permute-done.1
  22.9 1.3 collective-permute-start.2
  24.8 18.2 %all_gather.13 = bf16[384,1152]{1,0:T(8,128)(2,1)S(1)} all-gather(bf16[96,1152]{1,0:T(8,128)(2,1)} %param.14), channel_id=1, replica_groups=mesh['tm'=2,'space'=32,'dp'=4] {'dp'}, dimensions={0}, use_global_device_ids=true | all-gather | bytes 1105920 | tf_op jit(solution)/shard_map/all_gather | solution.py:58
  44.4 0.9 slice_dynamic-update-slice_fusion.22
  47.1 1.0 slice_dynamic-update-slice_fusion.19
  48.1 0.9 slice_dynamic-update-slice_fusion.18
  49.9 0.9 slice_dynamic-update-slice_fusion.16
  50.8 0.9 slice_dynamic-update-slice_fusion.15
  52.7 0.9 slice_dynamic-update-slice_fusion.13
  53.6 1.0 slice_dynamic-update-slice_fusion.12
  55.5 0.9 slice_dynamic-update-slice_fusion.10
  56.4 1.0 slice_dynamic-update-slice_fusion.9
  58.2 1.0 slice_dynamic-update-slice_fusion.7
  59.2 0.9 slice_dynamic-update-slice_fusion.6
  62.0 1.0 slice_dynamic-update-slice_fusion.4
  63.8 1.2 constant_dynamic-update-slice_fusion
  65.0 0.9 slice_dynamic-update-slice_fusion.2
  67.7 1.0 slice_dynamic-update-slice_fusion
  68.7 32.8 %all-gather.3.cloned.1.call-done = bf16[10368,384]{1,0:T(8,128)(2,1)} async-done(((bf16[2592,384]{1,0:T(8,128)(2,1)}), bf16[10368,384]{1,0:T(8,128)(2,1)}) %all-gather.3.cloned.1.call-update) | async-done | bytes 7962640 | tf_op jit(solution)/shard_map/all_gather | solution.py:75
  101.5 11.6 %fusion.24 = (f32[624]{0:T(1024)S(1)}, bf16[624,384]{1,0:T(8,128)(2,1)S(1)}) fusion(f32[384]{0:T(512)S(1)} %copy-done.3, bf16[624,10368]{1,0:T(8,128)(2,1)} %bitcast.4, bf16[10368,384]{1,0:T(8,128)(2,1)} %all-gather.3.cloned.1.call-done, bf16[624,384]{1,0:T(8,128)(2,1)S(1)} %bitcast.27), kind=kOutput, calls=%fused_computation.34 | convolution fusion | flops 4970354176 | bytes 21864384 | tf_op jit(solution)/shard_map/dot_general | solution.py:73
  113.1 1.7 convolution_convert_fusion
  114.8 10.1 %all_gather.15 = bf16[384,384]{1,0:T(8,128)(2,1)S(1)} all-gather(bf16[96,384]{1,0:T(8,128)(2,1)S(1)} %copy-done.1), channel_id=1, replica_groups=mesh['tm'=2,'space'=32,'dp'=4] {'dp'}, dimensions={0}, use_global_device_ids=true | all-gather | bytes 368640 | tf_op jit(solution)/shard_map/all_gather | solution.py:59
  125.4 206.7 %all-gather.5.cloned.1.call-done = bf16[3,6656,768]{2,1,0:T(8,128)(2,1)} async-done(((bf16[3,208,768]{2,1,0:T(8,128)(2,1)}), bf16[3,6656,768]{2,1,0:T(8,128)(2,1)}) %all-gather.5.cloned.1.call-update) | async-done | bytes 30670864 | tf_op jit(solution)/shard_map/all_gather | solution.py:91
  332.2 11.7 %fusion.3 = f32[3,208,6656]{2,1,0:T(8,128)} fusion(bf16[3,208,384]{2,1,0:T(8,128)(2,1)S(1)} %bitcast.30, bf16[3,6656,768]{2,1,0:T(8,128)(2,1)} %all-gather.5.cloned.1.call-done), kind=kOutput, calls=%fused_computation.5 | convolution fusion | flops 3189768192 | bytes 32428032 | tf_op jit(solution)/shard_map/fqc,fkc->fqk/dot_general | solution.py:95
  343.9 20.7 %fusion.39 = (f32[3,208]{1,0:T(4,128)S(1)}, f32[3,208,6656]{2,1,0:T(8,128)}) fusion(f32[3,208,6656]{2,1,0:T(8,128)} %fusion.3), kind=kOutput, calls=%fused_computation.81 | output fusion | flops 16620031 | bytes 33229248 | tf_op jit(solution)/shard_map/sub | solution.py:96
  364.6 13.4 %fusion.13 = bf16[3,208,384]{2,1,0:T(8,128)(2,1)S(1)} fusion(bf16[3,6656,768]{2,1,0:T(8,128)(2,1)} %all-gather.5.cloned.1.call-done, f32[3,208,6656]{2,1,0:T(8,128)} %get-tuple-element.14, f32[3,208]{1,0:T(4,128)S(1)} %get-tuple-element.13), kind=kOutput, calls=%fused_computation.23 | convolution fusion | flops 3198314496 | bytes 32430528 | tf_op jit(solution)/shard_map/fqk,fkc->fqc/dot_general | solution.py:98
  378.0 1.3 fusion.12
  (37 shorter events, 13.7 us)
Async XLA Ops:
  6.5 95.0 %all-gather.3.cloned.1.call-start = ((), (), s32[]{:S(2)}) async-start(), calls=%async_computation | async-start | bytes 9953280 | tf_op jit(solution)/shard_map/all_gather | solution.py:75
  7.3 324.9 %all-gather.5.cloned.1.call-start = ((), (), s32[]{:S(2)}) async-start(), calls=%async_computation.1 | async-start | bytes 31629312 | tf_op jit(solution)/shard_map/all_gather | solution.py:91
  10.0 8.4 %collective-permute-start = (bf16[3,1,104,384]{3,2,1,0:T(8,128)(2,1)S(1)}, bf16[3,1,104,384]{3,2,1,0:T(8,128)(2,1)S(1)}, u32[]{:S(2)}, u32[]{:S(2)}) collective-permute-start(bf16[3,1,104,384]{3,2,1,0:T(8,128)(2,1)S(1)} %get-tuple-element.7), channel_id=1, source_target_pairs={{0,4},{4,8},{8,12},{12,16},{16,20},{20,24},{24,28},{28,32},{32,36}... | collective-permute-start | bytes 718856 | tf_op jit(solution)/shard_map/ppermute | solution.py:17
  14.0 8.3 %collective-permute-start.1 = (bf16[3,1,104,384]{3,2,1,0:T(8,128)(2,1)S(1)}, bf16[3,1,104,384]{3,2,1,0:T(8,128)(2,1)S(1)}, u32[]{:S(2)}, u32[]{:S(2)}) collective-permute-start(bf16[3,1,104,384]{3,2,1,0:T(8,128)(2,1)S(1)} %get-tuple-element.8), channel_id=1, source_target_pairs={{4,0},{8,4},{12,8},{16,12},{20,16},{24,20},{28,24},{32,28},{36,32}... | collective-permute-start | bytes 718856 | tf_op jit(solution)/shard_map/ppermute | solution.py:19
  22.9 20.2 %collective-permute-start.2 = (bf16[2,4,106,384]{3,1,2,0:T(4,128)(2,1)S(1)}, bf16[2,4,106,384]{3,1,2,0:T(4,128)(2,1)S(1)}, u32[]{:S(2)}, u32[]{:S(2)}) collective-permute-start(bf16[2,4,106,384]{3,1,2,0:T(4,128)(2,1)S(1)} %copy.11), channel_id=1, source_target_pairs={{0,128},{1,129},{2,130},{3,131},{4,132},{5,133},{6,134},{7,135},{8... | collective-permute-start | bytes 1953800 | tf_op jit(solution)/shard_map/ppermute | solution.py:29
  43.0 20.8 %copy-start = (bf16[1,3,2,104,384]{4,3,2,1,0:T(8,128)(2,1)S(1)}, bf16[1,3,2,104,384]{4,3,2,1,0:T(8,128)(2,1)}, u32[]{:S(2)}) copy-start(bf16[1,3,2,104,384]{4,3,2,1,0:T(8,128)(2,1)} %param.8) | copy-start | bytes 1437700
  43.0 20.8 %copy-start.2 = (f32[384]{0:T(512)S(1)}, f32[384]{0:T(512)}, u32[]{:S(2)}) copy-start(f32[384]{0:T(512)} %param.12) | copy-start | bytes 4612
  44.4 57.1 %copy-start.3 = (f32[384]{0:T(512)S(1)}, f32[384]{0:T(512)}, u32[]{:S(2)}) copy-start(f32[384]{0:T(512)} %param.11) | copy-start | bytes 4612
  101.5 11.6 %copy-start.4 = (f32[384]{0:T(512)S(1)}, f32[384]{0:T(512)}, u32[]{:S(2)}) copy-start(f32[384]{0:T(512)} %param.13) | copy-start | bytes 4612
  101.5 13.3 %copy-start.1 = (bf16[96,384]{1,0:T(8,128)(2,1)S(1)}, bf16[96,384]{1,0:T(8,128)(2,1)}, u32[]{:S(2)}) copy-start(bf16[96,384]{1,0:T(8,128)(2,1)} %param.15) | copy-start | bytes 221188
Sparse Core Ops, SparseCore 0:
  9.2 92.2 all-gather.2
  114.9 217.2 all-gather.4
where the time goes:
time: 386 us
  waiting for transfers between devices  247 us (64%)
  matrix products  40.2 us (10%)
  blocking collectives  28.3 us (7%)
  other arithmetic  27.7 us (7%)
  local copies, waits for them, and re-layouts  22.7 us (6%)
  between operations  13.5 us (3%)
  starting transfers between devices  6.58 us (2%)
    all_gather x1, waiting for transfers between devices, on_device(): frame_pairs = lax.all_gather(local_pairs, 'space', axis=1, tiled=True)  207 us
    all_gather x1, waiting for transfers between devices, on_device(): lax.all_gather(conv_weight, 'dp', axis=0, tiled=True)  32.8 us
    unnamed x33, local copies, waits for them, and re-layouts  21.2 us
    sub x1, other arithmetic, on_device(): shifted = jnp.exp(scores - jnp.max(scores, axis=-1, keepdims=True))  20.7 us
    all_gather x1, blocking collectives, on_device(): lax.all_gather(qkv_weight, 'dp', axis=0, tiled=True)  18.2 us
    dot_general x1, matrix products, on_device(): jnp.einsum('fqk,fkc->fqc', probs, values, preferred_element_type=jnp.floa...  13.4 us
    dot_general x1, matrix products, on_device(): jnp.einsum('fqc,fkc->fqk', query, keys, preferred_element_type=jnp.float32)  11.7 us
    dot_general x1, matrix products, on_device(): jnp.dot(patches, lax.all_gather(conv_weight, 'dp', axis=0, tiled=True), p...  11.6 us
  transfers between devices with their start and end apart: 5, of which 4 were waited for; matrix products, arithmetic and copies ran while one was open for 8% of the time, Pallas kernels for 0%

commit v1 on v0

--- a/solution.py
+++ b/solution.py
@@ -1,9 +1,19 @@
+import functools
+import math
+
 import jax
 import jax.numpy as jnp
 from jax import lax
+from jax.experimental import pallas as pl
+from jax.experimental.pallas import tpu as pltpu
 from jax.sharding import PartitionSpec as P
 
 EPS = 1e-06
+MESH = pl.DeviceIdType.MESH
+XS = 4
+ZS = 8
+BF = jnp.bfloat16
+F32 = jnp.float32
 
 
 def with_halo(cells, sides, width):
@@ -42,6 +52,249 @@
                 windows.append(source[:, tap_h : tap_h + rows, tap_w : tap_w + width, :])
     joined = jnp.concatenate(windows, axis=-1)
     return joined.reshape(-1, joined.shape[-1])
+
+
+def dot(a, b):
+    return jnp.dot(a, b, preferred_element_type=F32)
+
+
+def dot_t(a, b):
+    return lax.dot_general(a, b, (((1,), (1,)), ((), ())), preferred_element_type=F32)
+
+
+def attention_kernel(
+    hid, qkv, outw, gain, out,
+    nbuf, kb, qbuf, mbuf, lbuf, acc, obuf, rbuf,
+    home_send, ret_send, sib_send, left_send, right_send, on_send, recv, ret_recv,
+):
+    chans = hid.shape[-1]
+    t = lax.axis_index("tm")
+    space = lax.axis_index("space")
+    z, x = lax.div(space, XS), lax.rem(space, XS)
+    left, right, across = lax.rem(x + XS - 1, XS), lax.rem(x + 1, XS), lax.rem(x + 2, XS)
+    parity = lax.rem(z, 2)
+    same = t == parity
+
+    def dev(core, row, col):
+        return {"tm": core, "space": row * XS + col}
+
+    barrier = pltpu.get_barrier_semaphore()
+
+    def greet(core, row, col):
+        pl.semaphore_signal(barrier, inc=1, device_id=dev(core, row, col), device_id_type=MESH)
+
+    greet(1 - t, z, x)
+    greet(t, z, left)
+    greet(t, z, right)
+    for d in range(1, ZS):
+        for core in range(2):
+            greet(core, lax.rem(z + d, ZS), x)
+
+    for j in range(3):
+        nbuf[j] = rms_scale(hid[j], gain[...]).astype(BF)
+
+    pl.semaphore_wait(barrier, 3 + 2 * (ZS - 1))
+
+    def copy(src, dst, send, rec, device):
+        return pltpu.make_async_remote_copy(
+            src_ref=src, dst_ref=dst, send_sem=send, recv_sem=rec, device_id=device, device_id_type=MESH
+        )
+
+    def home_copy(j):
+        b = x * ZS + z
+        return copy(nbuf.at[j], kb.at[b], home_send.at[j], recv.at[b], dev(parity, 2 * j + t, x))
+
+    for j in range(3):
+        @pl.when(2 * j + t != z)
+        def _():
+            home_copy(j).start()
+
+    is_worker = z < 6
+
+    @pl.when(is_worker)
+    def _():
+        slot = lax.div(z, 2)
+
+        def row_of(i, mine):
+            first = jnp.where(same, (0, 2, 6, 4)[i], (1, 7, 3, 5)[i])
+            second = jnp.where(same, (1, 7, 3, 5)[i], (0, 2, 6, 4)[i])
+            return lax.rem(z + (first if mine else second), ZS)
+
+        def block(col, i, mine=True):
+            return col * ZS + row_of(i, mine)
+
+        def landed(b):
+            copy(kb.at[b], kb.at[b], sib_send.at[0], recv.at[b], dev(1 - t, z, x)).wait_recv()
+
+        def push(b, send, device):
+            return copy(kb.at[b], kb.at[b], send, recv.at[b], device)
+
+        sib, lft, rgt = dev(1 - t, z, x), dev(t, z, left), dev(t, z, right)
+        sent = []
+
+        def own(i):
+            b = block(x, i)
+            if i == 0:
+                @pl.when(same)
+                def _():
+                    kb[b] = nbuf[slot]
+
+                @pl.when(jnp.logical_not(same))
+                def _():
+                    landed(b)
+            else:
+                landed(b)
+            for c in (push(b, left_send.at[i], lft), push(b, right_send.at[i], rgt), push(b, sib_send.at[i], sib)):
+                c.start()
+                sent.append(c)
+
+        def beside(i):
+            for k, (col, on) in enumerate(((left, rgt), (right, lft))):
+                b = block(col, i)
+                landed(b)
+                if (i < 2) == (k == 0):
+                    c = push(b, on_send.at[i], on)
+                    c.start()
+                    sent.append(c)
+                c = push(b, sib_send.at[4 + 2 * i + k], sib)
+                c.start()
+                sent.append(c)
+
+        def far(i):
+            b = block(across, i)
+            landed(b)
+            c = push(b, sib_send.at[12 + i], sib)
+            c.start()
+            sent.append(c)
+
+        def others(col):
+            for i in range(4):
+                landed(block(col, i, False))
+
+        def project(i):
+            n = kb[block(x, i)]
+            q = dot(n, qkv[:, :chans]).astype(BF)
+            qk = dot_t(q, qkv[:, chans : 2 * chans]) * (math.log2(math.e) / math.sqrt(chans))
+            qbuf[i] = qk.astype(BF)
+
+        def attend(i, col, first):
+            keys = kb[pl.ds(col * ZS, ZS)].reshape(-1, chans)
+            s = dot_t(qbuf[i], keys)
+            top = jnp.max(s, axis=-1, keepdims=True)
+            if not first:
+                top = jnp.maximum(top, mbuf[i])
+            p = jnp.exp2(s - top)
+            total = jnp.sum(p, axis=-1, keepdims=True)
+            mixed = dot(p.astype(BF), keys)
+            if not first:
+                alpha = jnp.exp2(mbuf[i] - top)
+                total = total + lbuf[i] * alpha
+                mixed = mixed + acc[i] * alpha
+            mbuf[i] = top
+            lbuf[i] = total
+            acc[i] = mixed
+
+        def back(i):
+            return copy(
+                obuf.at[i], rbuf.at[slot], ret_send.at[i], ret_recv.at[slot], dev(parity, row_of(i, True), x)
+            )
+
+        def finish(i):
+            mixed = (acc[i] * (1.0 / lbuf[i])).astype(BF)
+            attended = dot(mixed, qkv[:, 2 * chans :]).astype(BF)
+            if i == 0:
+                @pl.when(same)
+                def _():
+                    rbuf[slot] = attended
+
+                @pl.when(jnp.logical_not(same))
+                def _():
+                    obuf[i] = attended
+                    back(i).start()
+            else:
+                obuf[i] = attended
+                back(i).start()
+
+        own(0)
+        own(1)
+        beside(0)
+        own(2)
+        beside(1)
+        own(3)
+        for i in range(4):
+            project(i)
+        others(x)
+        attend(0, x, True)
+        beside(2)
+        attend(1, x, True)
+        beside(3)
+        attend(2, x, True)
+        far(0)
+        attend(3, x, True)
+        others(left)
+        attend(0, left, False)
+        far(1)
+        attend(1, left, False)
+        attend(2, left, False)
+        far(2)
+        attend(3, left, False)
+        others(right)
+        attend(0, right, False)
+        far(3)
+        for i in range(1, 4):
+            attend(i, right, False)
+        others(across)
+        for i in range(4):
+            attend(i, across, False)
+            finish(i)
+        for c in sent:
+            c.wait_send()
+        for i in range(4):
+            if i == 0:
+                @pl.when(jnp.logical_not(same))
+                def _():
+                    back(i).wait_send()
+            else:
+                back(i).wait_send()
+
+    for j in range(3):
+        @pl.when(2 * j + t != z)
+        def _():
+            home_copy(j).wait_send()
+            copy(rbuf.at[j], rbuf.at[j], ret_send.at[0], ret_recv.at[j], dev(1 - t, z, x)).wait_recv()
+
+        out[j] = (hid[j].astype(F32) + dot(rbuf[j], outw[...])).astype(BF)
+
+
+def attention(hidden, qkv, outw, gain):
+    frames, pixels, chans = hidden.shape
+    vmem = pl.BlockSpec(memory_space=pltpu.VMEM)
+    dma = pltpu.SemaphoreType.DMA
+    return pl.pallas_call(
+        attention_kernel,
+        out_shape=jax.ShapeDtypeStruct(hidden.shape, BF),
+        in_specs=[vmem] * 4,
+        out_specs=vmem,
+        scratch_shapes=[
+            pltpu.VMEM((3, pixels, chans), BF),
+            pltpu.VMEM((XS * ZS, pixels, chans), BF),
+            pltpu.VMEM((4, pixels, chans), BF),
+            pltpu.VMEM((4, pixels, 1), F32),
+            pltpu.VMEM((4, pixels, 1), F32),
+            pltpu.VMEM((4, pixels, chans), F32),
+            pltpu.VMEM((4, pixels, chans), BF),
+            pltpu.VMEM((3, pixels, chans), BF),
+            dma((3,)), dma((4,)), dma((16,)), dma((4,)), dma((4,)), dma((4,)),
+            dma((XS * ZS,)), dma((3,)),
+        ],
+        compiler_params=pltpu.CompilerParams(
+            collective_id=1, has_side_effects=True, vmem_limit_bytes=48 * 1024 * 1024
+        ),
+        cost_estimate=pl.CostEstimate(
+            flops=4 * 4 * pixels * 32 * pixels * chans, bytes_accessed=4 * frames * pixels * chans,
+            transcendentals=4 * pixels * 32 * pixels,
+        ),
+    )(hidden, qkv, outw, gain.reshape(1, chans))
 
 
 def on_device(
@@ -78,31 +331,8 @@
     hidden = (local.reshape(frames * pixels, chans).astype(jnp.float32) + conv + conv_bias).astype(
         jnp.bfloat16
     )
-    normed = rms_scale(hidden, attn_gain).astype(jnp.bfloat16)
-    query = jnp.dot(normed, full_qkv[:, :chans], preferred_element_type=jnp.float32).astype(
-        jnp.bfloat16
-    )
-    query = query.reshape(frames, pixels, chans)
-    key_value_weight = full_qkv[:, chans:]
-    local_pairs = jnp.dot(normed, key_value_weight, preferred_element_type=jnp.float32).astype(
-        jnp.bfloat16
-    )
-    local_pairs = local_pairs.reshape(frames, pixels, 2 * chans)
-    frame_pairs = lax.all_gather(local_pairs, "space", axis=1, tiled=True)
-    keys = frame_pairs[:, :, :chans]
-    values = frame_pairs[:, :, chans:]
-    scale = 1.0 / jnp.sqrt(jnp.float32(chans))
-    scores = jnp.einsum("fqc,fkc->fqk", query, keys, preferred_element_type=jnp.float32) * scale
-    shifted = jnp.exp(scores - jnp.max(scores, axis=-1, keepdims=True))
-    probs = (shifted / jnp.sum(shifted, axis=-1, keepdims=True)).astype(jnp.bfloat16)
-    attended = jnp.einsum("fqk,fkc->fqc", probs, values, preferred_element_type=jnp.float32).astype(
-        jnp.bfloat16
-    )
-    attended = attended.reshape(frames * pixels, chans)
-    result = hidden.astype(jnp.float32) + jnp.dot(
-        attended, full_out, preferred_element_type=jnp.float32
-    )
-    return result.astype(jnp.bfloat16).reshape(1, frames, rows, width, chans)
+    result = attention(hidden.reshape(frames, pixels, chans), full_qkv, full_out, attn_gain)
+    return result.reshape(1, frames, rows, width, chans)
 
 
 def solution(mesh):

time: 386 us -> 203 us (0.53)
  waiting for transfers between devices: 247 us -> 30.5 us
  Pallas kernels: 0 us -> 78.4 us
  matrix products: 40.2 us -> 12.3 us
  other arithmetic: 27.7 us -> 6.9 us
    all_gather x1 -> x0, waiting for transfers between devices: 207 us -> none  [on_device(): frame_pairs = lax.all_gather(local_pairs, 'space', axis=1, tiled=True)]
    pallas_call x0 -> x1, Pallas kernels: none -> 78.4 us  [attention(): pl.pallas_call(attention_kernel, out_shape=jax.ShapeDtypeStruct(hidden.sh...]
    dot_general x5 -> x0, matrix products: 28.6 us -> none  [the longest x1 13.4 us: on_device(): jnp.einsum('fqk,fkc->fqc', probs, values, preferred_element_type=jnp.floa...]
    sub x1 -> x0, other arithmetic: 20.7 us -> none  [on_device(): shifted = jnp.exp(scores - jnp.max(scores, axis=-1, keepdims=True))]
    all_gather x1, waiting for transfers between devices: 32.8 us -> 23.5 us  [on_device(): lax.all_gather(conv_weight, 'dp', axis=0, tiled=True)]
    unnamed x33 -> x30, local copies, waits for them, and re-layouts: 21.2 us -> 21.9 us
  transfers between devices with their start and end apart: 5 -> 4, of which waited for: 4 -> 3; matrix products, arithmetic and copies ran while one was open for 8% -> 15% of each run, Pallas kernels for 0% -> 0%
where the time goes in v1:
time: 203 us
  Pallas kernels  78.4 us (39%)
  blocking collectives  30.6 us (15%)
  waiting for transfers between devices  30.5 us (15%)
  local copies, waits for them, and re-layouts  24 us (12%)
  between operations  13.5 us (7%)
  matrix products  12.3 us (6%)
  other arithmetic  6.9 us (3%)
  starting transfers between devices  6.55 us (3%)
    pallas_call x1, Pallas kernels, attention(): pl.pallas_call(attention_kernel, out_shape=jax.ShapeDtypeStruct(hidden.sh...  78.4 us
    all_gather x1, waiting for transfers between devices, on_device(): lax.all_gather(conv_weight, 'dp', axis=0, tiled=True)  23.5 us
    unnamed x30, local copies, waits for them, and re-layouts  21.9 us
    all_gather x1, blocking collectives, on_device(): lax.all_gather(qkv_weight, 'dp', axis=0, tiled=True)  18.6 us
    dot_general x1, matrix products, on_device(): jnp.dot(patches, lax.all_gather(conv_weight, 'dp', axis=0, tiled=True), p...  12.3 us
    all_gather x1, blocking collectives, on_device(): lax.all_gather(out_weight, 'dp', axis=0, tiled=True)  12 us
  transfers between devices with their start and end apart: 4, of which 3 were waited for; matrix products, arithmetic and copies ran while one was open for 15% of the time, Pallas kernels for 0%

profile of v1, /device:TPU:1, one launch (start us, length us, event | category | flops | bytes accessed | tf_op | source)
XLA Modules:
  0.0 202.7 jit_solution(12498193366158674698)
XLA Ops:
  7.3 1.2 fusion.11
  8.5 1.4 multiply_convert_fusion
  9.9 4.0 %collective-permute-start = (bf16[3,1,104,384]{3,2,1,0:T(8,128)(2,1)S(1)}, bf16[3,1,104,384]{3,2,1,0:T(8,128)(2,1)S(1)}, u32[]{:S(2)}, u32[]{:S(2)}) collective-permute-start(bf16[3,1,104,384]{3,2,1,0:T(8,128)(2,1)S(1)} %get-tuple-element.7), channel_id=1, source_target_pairs={{0,4},{4,8},{8,12},{12,16},{16,20},{20,24},{24,28},{28,32},{32,36}... | collective-permute-start | bytes 718856 | tf_op jit(solution)/shard_map/ppermute | solution.py:27
  13.9 1.3 collective-permute-start.1
  15.9 2.5 %collective-permute-done = bf16[3,1,104,384]{3,2,1,0:T(8,128)(2,1)S(1)} collective-permute-done((bf16[3,1,104,384]{3,2,1,0:T(8,128)(2,1)S(1)}, bf16[3,1,104,384]{3,2,1,0:T(8,128)(2,1)S(1)}, u32[]{:S(2)}, u32[]{:S(2)}) %collective-permute-start) | collective-permute-done | bytes 239648 | tf_op jit(solution)/shard_map/ppermute | solution.py:27
  18.4 3.8 %collective-permute-done.1 = bf16[3,1,104,384]{3,2,1,0:T(8,128)(2,1)S(1)} collective-permute-done((bf16[3,1,104,384]{3,2,1,0:T(8,128)(2,1)S(1)}, bf16[3,1,104,384]{3,2,1,0:T(8,128)(2,1)S(1)}, u32[]{:S(2)}, u32[]{:S(2)}) %collective-permute-start.1) | collective-permute-done | bytes 239648 | tf_op jit(solution)/shard_map/ppermute | solution.py:29
  22.8 1.3 collective-permute-start.2
  24.1 12.0 %all_gather.11.outw = bf16[384,384]{1,0:T(8,128)(2,1)S(1)} all-gather(bf16[96,384]{1,0:T(8,128)(2,1)} %param.15), channel_id=1, replica_groups=mesh['tm'=2,'space'=32,'dp'=4] {'dp'}, dimensions={0}, use_global_device_ids=true | all-gather | bytes 368640 | tf_op jit(solution)/shard_map/all_gather | solution.py:312
  36.8 18.6 %all_gather.10.qkv = bf16[384,1152]{1,0:T(8,128)(2,1)S(1)} all-gather(bf16[96,1152]{1,0:T(8,128)(2,1)} %param.14), channel_id=1, replica_groups=mesh['tm'=2,'space'=32,'dp'=4] {'dp'}, dimensions={0}, use_global_device_ids=true | all-gather | bytes 1105920 | tf_op jit(solution)/shard_map/all_gather | solution.py:311
  56.7 0.9 slice_dynamic-update-slice_fusion.22
  57.7 0.9 slice_dynamic-update-slice_fusion.21
  59.5 1.0 slice_dynamic-update-slice_fusion.19
  60.4 1.0 slice_dynamic-update-slice_fusion.18
  61.4 0.9 slice_dynamic-update-slice_fusion.17
  62.3 0.9 slice_dynamic-update-slice_fusion.16
  63.3 1.0 slice_dynamic-update-slice_fusion.15
  65.1 1.0 slice_dynamic-update-slice_fusion.13
  66.1 0.9 slice_dynamic-update-slice_fusion.12
  67.8 0.9 slice_dynamic-update-slice_fusion.10
  68.8 0.9 slice_dynamic-update-slice_fusion.9
  69.7 0.9 slice_dynamic-update-slice_fusion.8
  70.6 0.9 slice_dynamic-update-slice_fusion.7
  71.5 0.9 slice_dynamic-update-slice_fusion.6
  73.3 0.9 fusion.14
  74.2 1.0 slice_dynamic-update-slice_fusion.4
  76.0 1.2 constant_dynamic-update-slice_fusion
  77.2 1.0 slice_dynamic-update-slice_fusion.2
  79.1 0.9 fusion.13
  80.0 0.9 slice_dynamic-update-slice_fusion
  80.9 23.5 %all-gather.2.cloned.1.call-done = bf16[10368,384]{1,0:T(8,128)(2,1)} async-done(((bf16[2592,384]{1,0:T(8,128)(2,1)}), bf16[10368,384]{1,0:T(8,128)(2,1)}) %all-gather.2.cloned.1.call-update) | async-done | bytes 7962640 | tf_op jit(solution)/shard_map/all_gather | solution.py:328
  104.4 12.3 %fusion.2 = bf16[624,384]{1,0:T(8,128)(2,1)S(1)} fusion(bf16[624,10368]{1,0:T(8,128)(2,1)} %bitcast.4, bf16[10368,384]{1,0:T(8,128)(2,1)} %all-gather.2.cloned.1.call-done, f32[384]{0:T(512)S(1)} %copy-done.2, bf16[624,384]{1,0:T(8,128)(2,1)S(1)} %bitcast.24), kind=kOutput, calls=%fused_computation.7 | convolution fusion | flops 4969635840 | bytes 21861888 | tf_op jit(solution)/shard_map/dot_general | solution.py:326
  116.7 78.4 %shard_map.82 = bf16[3,208,384]{2,1,0:T(8,128)(2,1)S(1)} custom-call(bf16[3,208,384]{2,1,0:T(8,128)(2,1)S(1)} %bitcast.23, bf16[384,1152]{1,0:T(8,128)(2,1)S(1)} %all_gather.10.qkv, bf16[384,384]{1,0:T(8,128)(2,1)S(1)} %all_gather.11.outw, f32[1,384]{1,0:T(1,128)S(1)} %reshape.48.gain), custom_call_target="tpu_custom_call" | custom-call | flops 8506048512 | bytes 958464 | tf_op jit(solution)/shard_map/pallas_call | solution.py:273
  (26 shorter events, 10.0 us)
Async XLA Ops:
  6.5 97.8 %all-gather.2.cloned.1.call-start = ((), (), s32[]{:S(2)}) async-start(), calls=%async_computation | async-start | bytes 9953280 | tf_op jit(solution)/shard_map/all_gather | solution.py:328
  9.9 8.4 %collective-permute-start = (bf16[3,1,104,384]{3,2,1,0:T(8,128)(2,1)S(1)}, bf16[3,1,104,384]{3,2,1,0:T(8,128)(2,1)S(1)}, u32[]{:S(2)}, u32[]{:S(2)}) collective-permute-start(bf16[3,1,104,384]{3,2,1,0:T(8,128)(2,1)S(1)} %get-tuple-element.7), channel_id=1, source_target_pairs={{0,4},{4,8},{8,12},{12,16},{16,20},{20,24},{24,28},{28,32},{32,36}... | collective-permute-start | bytes 718856 | tf_op jit(solution)/shard_map/ppermute | solution.py:27
  13.9 8.3 %collective-permute-start.1 = (bf16[3,1,104,384]{3,2,1,0:T(8,128)(2,1)S(1)}, bf16[3,1,104,384]{3,2,1,0:T(8,128)(2,1)S(1)}, u32[]{:S(2)}, u32[]{:S(2)}) collective-permute-start(bf16[3,1,104,384]{3,2,1,0:T(8,128)(2,1)S(1)} %get-tuple-element.8), channel_id=1, source_target_pairs={{4,0},{8,4},{12,8},{16,12},{20,16},{24,20},{28,24},{32,28},{36,32}... | collective-permute-start | bytes 718856 | tf_op jit(solution)/shard_map/ppermute | solution.py:29
  22.8 32.6 %collective-permute-start.2 = (bf16[2,4,106,384]{3,1,2,0:T(4,128)(2,1)S(1)}, bf16[2,4,106,384]{3,1,2,0:T(4,128)(2,1)S(1)}, u32[]{:S(2)}, u32[]{:S(2)}) collective-permute-start(bf16[2,4,106,384]{3,1,2,0:T(4,128)(2,1)S(1)} %copy.11), channel_id=1, source_target_pairs={{0,128},{1,129},{2,130},{3,131},{4,132},{5,133},{6,134},{7,135},{8... | collective-permute-start | bytes 1953800 | tf_op jit(solution)/shard_map/ppermute | solution.py:39
  55.4 20.6 %copy-start = (bf16[1,3,2,104,384]{4,3,2,1,0:T(8,128)(2,1)S(1)}, bf16[1,3,2,104,384]{4,3,2,1,0:T(8,128)(2,1)}, u32[]{:S(2)}) copy-start(bf16[1,3,2,104,384]{4,3,2,1,0:T(8,128)(2,1)} %param.8) | copy-start | bytes 1437700
  55.4 20.6 %copy-start.1 = (f32[384]{0:T(512)S(1)}, f32[384]{0:T(512)}, u32[]{:S(2)}) copy-start(f32[384]{0:T(512)} %param.12) | copy-start | bytes 4612
  56.7 47.6 %copy-start.2 = (f32[384]{0:T(512)S(1)}, f32[384]{0:T(512)}, u32[]{:S(2)}) copy-start(f32[384]{0:T(512)} %param.11) | copy-start | bytes 4612
Sparse Core Ops, SparseCore 0:
  9.2 95.1 all-gather.1

commit v2 on v1

--- a/solution.py
+++ b/solution.py
@@ -16,42 +16,9 @@
 F32 = jnp.float32
 
 
-def with_halo(cells, sides, width):
-    for axis, dim in sides:
-        count = lax.axis_size(axis)
-        ends = count - 1
-        head = lax.slice_in_dim(cells, 0, width, axis=dim)
-        tail = lax.slice_in_dim(cells, cells.shape[dim] - width, cells.shape[dim], axis=dim)
-        cells = jnp.concatenate(
-            [
-                lax.ppermute(tail, axis, [(i, (i + 1) % count) for i in range(ends)]),
-                cells,
-                lax.ppermute(head, axis, [((i + 1) % count, i) for i in range(ends)]),
-            ],
-            axis=dim,
-        )
-    return cells
-
-
-def passed_along(value, axis, steps):
-    count = lax.axis_size(axis)
-    first, last = (max(0, -steps), min(count, count - steps))
-    return lax.ppermute(value, axis, [(source, source + steps) for source in range(first, last)])
-
-
 def rms_scale(values, gain):
     values = values.astype(jnp.float32)
     return values * lax.rsqrt(jnp.mean(values * values, axis=-1, keepdims=True) + EPS) * gain
-
-
-def build_patches(sources, rows, width):
-    windows = []
-    for source in sources:
-        for tap_h in range(3):
-            for tap_w in range(3):
-                windows.append(source[:, tap_h : tap_h + rows, tap_w : tap_w + width, :])
-    joined = jnp.concatenate(windows, axis=-1)
-    return joined.reshape(-1, joined.shape[-1])
 
 
 def dot(a, b):
@@ -297,42 +264,321 @@
     )(hidden, qkv, outw, gain.reshape(1, chans))
 
 
+QUARTER = 2592
+HALF = 1280
+PART = 640
+XPIECE = PART // XS
+ZPIECE = PART // ZS
+REST = 16
+WIDE = 112
+
+
+def conv_kernel(
+    feat, fidx, w, qkvw, ow, bias, gain, hid, qkv_out, ow_out,
+    wb, qb, ob, u, lhs, acc,
+    local_sem, y_send, y_recv, x_send, x_on, x_recv, z_send, z_on, z_recv, s_send, s_recv,
+    h_send, h_recv,
+):
+    chans = feat.shape[-1]
+    width = feat.shape[-2]
+    t = lax.axis_index("tm")
+    space = lax.axis_index("space")
+    y = lax.axis_index("dp")
+    z, x = lax.div(space, XS), lax.rem(space, XS)
+    left, right, across = lax.rem(x + XS - 1, XS), lax.rem(x + 1, XS), lax.rem(x + 2, XS)
+    down, up = lax.rem(z + ZS - 1, ZS), lax.rem(z + 1, ZS)
+    before, after = lax.rem(space + 31, 32), lax.rem(space + 1, 32)
+
+    def dev(core, row, col):
+        return {"tm": core, "space": row * XS + col}
+
+    sib, lft, rgt = dev(1 - t, z, x), dev(t, z, left), dev(t, z, right)
+    dwn, upw = dev(t, down, x), dev(t, up, x)
+    barrier = pltpu.get_barrier_semaphore()
+
+    def greet(device):
+        pl.semaphore_signal(barrier, inc=1, device_id=device, device_id_type=MESH)
+
+    for d in range(1, 4):
+        greet({"dp": lax.rem(y + d, 4)})
+    for device in (sib, lft, rgt, dwn, upw):
+        greet(device)
+    for core in range(2):
+        greet({"tm": core, "space": before})
+        greet({"tm": core, "space": after})
+
+    def copy(src, dst, send, rec, device):
+        return pltpu.make_async_remote_copy(
+            src_ref=src, dst_ref=dst, send_sem=send, recv_sem=rec, device_id=device, device_id_type=MESH
+        )
+
+    def rows(start, count):
+        return pl.ds(pl.multiple_of(start, 16), count)
+
+    mine = pltpu.make_async_copy(w, wb.at[rows(y * QUARTER, QUARTER)], local_sem)
+    mine.start()
+
+    pad = jnp.zeros((WIDE - width, chans), F32)
+    for f in range(3):
+        for r in range(2):
+            scaled = rms_scale(feat[0, f, r], gain[...])
+            act = scaled * jax.nn.sigmoid(scaled)
+            u[1 + r, 2 + f] = jnp.concatenate([act, pad], axis=0).astype(BF)
+    blank = jnp.zeros((3, WIDE, chans), BF)
+
+    @pl.when(space == 0)
+    def _():
+        u[0, 2:5] = blank
+        u[0, 0:2] = blank[:2]
+
+    @pl.when(space == 31)
+    def _():
+        u[3, 2:5] = blank
+        u[3, 0:2] = blank[:2]
+
+    @pl.when(t == 0)
+    def _():
+        for r in range(4):
+            u[r, 0:2] = blank[:2]
+
+    pl.semaphore_wait(barrier, 12)
+
+    sent = []
+
+    def go(c):
+        c.start()
+        sent.append(c)
+
+    def x_rows(j, col):
+        return rows(j * QUARTER + t * HALF + col * XPIECE, XPIECE)
+
+    def z_rows(j, row):
+        return rows(j * QUARTER + t * HALF + PART + row * ZPIECE, ZPIECE)
+
+    def rest_rows(j, core):
+        return rows(j * QUARTER + 2 * HALF + core * REST, REST)
+
+    def half_rows(core):
+        return rows(core * 48, 48)
+
+    owner = [lax.rem(y + d, 4) for d in (3, 1, 2)]
+    target = [{"dp": lax.rem(y + d, 4)} for d in (1, 3, 2)]
+    for k in range(3):
+        src = w.at[rows(t * HALF + x * XPIECE, XPIECE)]
+        go(copy(src, wb.at[x_rows(y, x)], y_send.at[k, 0], y_recv.at[k, 0], target[k]))
+        src = w.at[rows(t * HALF + PART + z * ZPIECE, ZPIECE)]
+        go(copy(src, wb.at[z_rows(y, z)], y_send.at[k, 1], y_recv.at[k, 1], target[k]))
+
+    def rim(src, dst, n, device):
+        return copy(src, dst, h_send.at[n], h_recv.at[n], device)
+
+    rims = (
+        (space < 31, rim(u.at[2, 2:5], u.at[0, 2:5], 0, {"space": after})),
+        (space > 0, rim(u.at[1, 2:5], u.at[3, 2:5], 1, {"space": before})),
+        (t == 0, rim(u.at[1:3, 3:5], u.at[1:3, 0:2], 2, {"tm": 1 - t})),
+        (jnp.logical_and(t == 0, space < 31), rim(u.at[2, 3:5], u.at[0, 0:2], 3, {"tm": 1 - t, "space": after})),
+        (jnp.logical_and(t == 0, space > 0), rim(u.at[1, 3:5], u.at[3, 0:2], 4, {"tm": 1 - t, "space": before})),
+    )
+    for cond, c in rims:
+        pl.when(cond)(c.start)
+
+    for k in range(3):
+        src = w.at[rows(2 * HALF + t * REST, REST)]
+        go(copy(src, wb.at[rest_rows(y, t)], y_send.at[k, 2], y_recv.at[k, 2], target[k]))
+        go(copy(qkvw.at[half_rows(t)], qb.at[y, half_rows(t)], y_send.at[k, 3], y_recv.at[k, 3], target[k]))
+        go(copy(ow.at[half_rows(t)], ob.at[y, half_rows(t)], y_send.at[k, 4], y_recv.at[k, 4], target[k]))
+
+    def landed(ref, sem):
+        copy(ref, ref, s_send.at[0, 0], sem, sib).wait_recv()
+
+    def push(ref, send, rec, device):
+        go(copy(ref, ref, send, rec, device))
+
+    def from_y(k):
+        ref = wb.at[x_rows(owner[k], x)]
+        landed(ref, y_recv.at[k, 0])
+        push(ref, x_send.at[k, 0], x_recv.at[k, 0], rgt)
+        push(ref, x_send.at[k, 1], x_recv.at[k, 1], lft)
+        ref = wb.at[z_rows(owner[k], z)]
+        landed(ref, y_recv.at[k, 1])
+        push(ref, z_send.at[k, 0], z_recv.at[k, 0], upw)
+        push(ref, z_send.at[k, 1], z_recv.at[k, 1], dwn)
+
+    def x_one(k):
+        for way, (col, on) in enumerate(((left, rgt), (right, lft))):
+            ref = wb.at[x_rows(owner[k], col)]
+            landed(ref, x_recv.at[k, way])
+            if way == k % 2:
+                push(ref, x_on.at[k], x_recv.at[k, 2], on)
+
+    def x_two(k):
+        landed(wb.at[x_rows(owner[k], across)], x_recv.at[k, 2])
+        push(wb.at[rows(owner[k] * QUARTER + t * HALF, PART)], s_send.at[k, 0], s_recv.at[k, 0], sib)
+
+    def z_step(k, d):
+        for way, on in enumerate((upw, dwn)):
+            row = lax.rem(z + (ZS - d if way == 0 else d), ZS)
+            ref = wb.at[z_rows(owner[k], row)]
+            landed(ref, z_recv.at[k, 2 * d - 2 + way])
+            if d < 3:
+                push(ref, z_on.at[k, 2 * d - 2 + way], z_recv.at[k, 2 * d + way], on)
+            elif way == k % 2:
+                push(ref, z_on.at[k, 4], z_recv.at[k, 6], on)
+
+    def z_last(k):
+        landed(wb.at[z_rows(owner[k], lax.rem(z + 4, ZS))], z_recv.at[k, 6])
+        push(wb.at[rows(owner[k] * QUARTER + t * HALF + PART, PART)], s_send.at[k, 1], s_recv.at[k, 1], sib)
+
+    def small(k):
+        for n, ref in enumerate(
+            (wb.at[rest_rows(owner[k], t)], qb.at[owner[k], half_rows(t)], ob.at[owner[k], half_rows(t)])
+        ):
+            landed(ref, y_recv.at[k, 2 + n])
+            push(ref, s_send.at[k, 2 + n], s_recv.at[k, 2 + n], sib)
+
+    def shared(k):
+        start = owner[k] * QUARTER + (1 - t) * HALF
+        landed(wb.at[rows(start, PART)], s_recv.at[k, 0])
+        landed(wb.at[rows(start + PART, PART)], s_recv.at[k, 1])
+        landed(wb.at[rest_rows(owner[k], 1 - t)], s_recv.at[k, 2])
+
+    keep = [
+        [(fidx[0, f] >= 2 - kt).astype(F32) for f in range(3)] for kt in range(2)
+    ]
+
+    def spread(g, r):
+        cells = u[r, g].astype(F32)
+        for kw in range(3):
+            moved = cells if kw == 1 else pltpu.roll(cells, 1 if kw == 0 else WIDE - 1, 0)
+            for kt in range(3):
+                f = g - kt
+                if 0 <= f < 3:
+                    lhs[kt * 3 + kw, f, r] = (moved if kt == 2 else moved * keep[kt][f]).astype(BF)
+
+    def tap(number):
+        kt, kh, kw = number // 9, (number // 3) % 3, number % 3
+        if not isinstance(number, int):
+            kt, kh, kw = lax.div(number, 9), lax.rem(lax.div(number, 3), 3), lax.rem(number, 3)
+        cells = lhs[kt * 3 + kw, :, pl.ds(kh, 2)].reshape(-1, chans)
+        acc[...] += dot(cells, wb[rows(number * chans, chans)])
+
+    def taps(j, first, last):
+        @pl.loop(first, last)
+        def _(i):
+            tap(7 * j + i)
+
+    for g in range(2, 5):
+        for r in range(1, 3):
+            spread(g, r)
+    from_y(0)
+    from_y(1)
+    x_one(0)
+    z_step(0, 1)
+    from_y(2)
+    for n, cond in enumerate(
+        (space > 0, space < 31, t == 1, jnp.logical_and(t == 1, space > 0), jnp.logical_and(t == 1, space < 31))
+    ):
+        pl.when(cond)(rims[n][1].wait_recv)
+    for g in range(2, 5):
+        spread(g, 0)
+        spread(g, 3)
+    z_step(0, 2)
+    x_one(1)
+    z_step(1, 1)
+    for g in range(2):
+        for r in range(4):
+            spread(g, r)
+    x_two(0)
+    z_step(0, 3)
+    z_step(1, 2)
+    x_one(2)
+    z_step(2, 1)
+    acc[...] = jnp.zeros_like(acc)
+    mine.wait()
+    taps(y, 0, 2)
+    x_two(1)
+    z_last(0)
+    z_step(1, 3)
+    z_step(2, 2)
+    taps(y, 2, 4)
+    x_two(2)
+    z_last(1)
+    z_step(2, 3)
+    taps(y, 4, 6)
+    for k in range(3):
+        small(k)
+    z_last(2)
+    for k in range(3):
+        shared(k)
+        taps(owner[k], 0, 6)
+    for number in (6, 13, 20):
+        tap(number)
+
+    for f in range(3):
+        both = []
+        for r in range(2):
+            part = acc[pl.ds((f * 2 + r) * WIDE, width)]
+            both.append(feat[0, f, r].astype(F32) + part + bias[...])
+        hid[f] = jnp.concatenate(both, axis=0).astype(BF)
+
+    for k in range(3):
+        landed(qb.at[owner[k], half_rows(1 - t)], s_recv.at[k, 3])
+        landed(ob.at[owner[k], half_rows(1 - t)], s_recv.at[k, 4])
+    for j in range(4):
+        qkv_out[pl.ds(96 * j, 96)] = qb[j]
+        ow_out[pl.ds(96 * j, 96)] = ob[j]
+    mine_rows = rows(96 * y, 96)
+    qkv_out[mine_rows] = qkvw[...]
+    ow_out[mine_rows] = ow[...]
+
+    for c in sent:
+        c.wait_send()
+    for cond, c in rims:
+        pl.when(cond)(c.wait_send)
+
+
+def convolution(feat, fidx, w, qkvw, ow, bias, gain):
+    chans = feat.shape[-1]
+    vmem = pl.BlockSpec(memory_space=pltpu.VMEM)
+    smem = pl.BlockSpec(memory_space=pltpu.SMEM)
+    hbm = pl.BlockSpec(memory_space=pl.ANY)
+    dma = pltpu.SemaphoreType.DMA
+    return pl.pallas_call(
+        conv_kernel,
+        out_shape=(
+            jax.ShapeDtypeStruct((3, 208, chans), BF),
+            jax.ShapeDtypeStruct((chans, 3 * chans), BF),
+            jax.ShapeDtypeStruct((chans, chans), BF),
+        ),
+        in_specs=[vmem, smem, hbm, vmem, vmem, vmem, vmem],
+        out_specs=(vmem,) * 3,
+        scratch_shapes=[
+            pltpu.VMEM((4 * QUARTER, chans), BF),
+            pltpu.VMEM((4, 96, 3 * chans), BF),
+            pltpu.VMEM((4, 96, chans), BF),
+            pltpu.VMEM((4, 5, WIDE, chans), BF),
+            pltpu.VMEM((9, 3, 4, WIDE, chans), BF),
+            pltpu.VMEM((6 * WIDE, chans), F32),
+            dma, dma((3, 5)), dma((3, 5)), dma((3, 2)), dma((3,)), dma((3, 3)),
+            dma((3, 2)), dma((3, 5)), dma((3, 7)), dma((3, 5)), dma((3, 5)),
+            dma((5,)), dma((5,)),
+        ],
+        compiler_params=pltpu.CompilerParams(
+            collective_id=2, has_side_effects=True, vmem_limit_bytes=48 * 1024 * 1024
+        ),
+        cost_estimate=pl.CostEstimate(
+            flops=2 * 624 * 27 * chans * chans, bytes_accessed=4 * QUARTER * chans * 2, transcendentals=0
+        ),
+    )(feat, fidx, w, qkvw, ow, bias.reshape(1, chans), gain.reshape(1, chans))
+
+
 def on_device(
     features, frame_index, conv_weight, conv_bias, norm_gain, attn_gain, qkv_weight, out_weight
 ):
-    frames, rows, width, chans = (
-        features.shape[1],
-        features.shape[2],
-        features.shape[3],
-        features.shape[4],
+    hidden, full_qkv, full_out = convolution(
+        features, frame_index, conv_weight, qkv_weight, out_weight, conv_bias, norm_gain
     )
-    pixels = rows * width
-    full_qkv, full_out = (
-        lax.all_gather(qkv_weight, "dp", axis=0, tiled=True),
-        lax.all_gather(out_weight, "dp", axis=0, tiled=True),
-    )
-    local = features[0]
-    activated = jax.nn.silu(rms_scale(local, norm_gain)).astype(jnp.bfloat16)
-    rimmed = with_halo(activated, (("space", 1),), 1)
-    rimmed = jnp.pad(rimmed, ((0, 0), (0, 0), (1, 1), (0, 0)))
-    prior = passed_along(rimmed[frames - 2 :], "tm", 1)
-    sequence = jnp.concatenate([prior, rimmed], axis=0)
-    position = frame_index[0]
-    keep_one = (position >= 1).astype(jnp.bfloat16)[:, None, None, None]
-    keep_two = (position >= 2).astype(jnp.bfloat16)[:, None, None, None]
-    earlier = sequence[1 : frames + 1] * keep_one
-    oldest = sequence[:frames] * keep_two
-    patches = build_patches((oldest, earlier, rimmed), rows, width)
-    conv = jnp.dot(
-        patches,
-        lax.all_gather(conv_weight, "dp", axis=0, tiled=True),
-        preferred_element_type=jnp.float32,
-    )
-    hidden = (local.reshape(frames * pixels, chans).astype(jnp.float32) + conv + conv_bias).astype(
-        jnp.bfloat16
-    )
-    result = attention(hidden.reshape(frames, pixels, chans), full_qkv, full_out, attn_gain)
-    return result.reshape(1, frames, rows, width, chans)
+    return attention(hidden, full_qkv, full_out, attn_gain).reshape(features.shape)
 
 
 def solution(mesh):

time: 203 us -> 140 us (0.69)
  Pallas kernels: 78.4 us -> 131 us
  blocking collectives: 30.6 us -> 0 us
  waiting for transfers between devices: 30.5 us -> 0 us
  local copies, waits for them, and re-layouts: 24 us -> 7.88 us
  between operations: 13.5 us -> 0.02 us
  matrix products: 12.3 us -> 0 us
  other arithmetic: 6.9 us -> 0 us
  starting transfers between devices: 6.55 us -> 0 us
    pallas_call x0 -> x1, Pallas kernels: none -> 54.9 us  [convolution(): pl.pallas_call(conv_kernel, out_shape=(jax.ShapeDtypeStruct((3, 208, chan...]
    all_gather x2 -> x0, blocking collectives: 30.6 us -> none  [the longest x1 18.6 us: on_device(): lax.all_gather(qkv_weight, 'dp', axis=0, tiled=True)]
    all_gather x1 -> x0, waiting for transfers between devices: 23.5 us -> none  [on_device(): lax.all_gather(conv_weight, 'dp', axis=0, tiled=True)]
    unnamed x30 -> x11, local copies, waits for them, and re-layouts: 21.9 us -> 5.83 us
    dot_general x1 -> x0, matrix products: 12.3 us -> none  [on_device(): jnp.dot(patches, lax.all_gather(conv_weight, 'dp', axis=0, tiled=True), p...]
    ppermute x3 -> x0, starting transfers between devices: 6.54 us -> none  [the longest x1 3.96 us: with_halo(): lax.ppermute(tail, axis, [(i, (i + 1) % count) for i in range(ends)])]
    ppermute x3 -> x0, waiting for transfers between devices: 6.28 us -> none  [the longest x1 3.81 us: with_halo(): lax.ppermute(head, axis, [((i + 1) % count, i) for i in range(ends)])]
    unnamed x3 -> x0, other arithmetic: 2.97 us -> none
  transfers between devices with their start and end apart: 4 -> 0, of which waited for: 3 -> 0; matrix products, arithmetic and copies ran while one was open for 15% -> 0% of each run, Pallas kernels for 0% -> 0%
where the time goes in v2:
time: 140 us; the launch traced here: 139 us
  Pallas kernels  131 us (94%)
  local copies, waits for them, and re-layouts  7.88 us (6%)
    pallas_call x1, Pallas kernels, attention(): pl.pallas_call(attention_kernel, out_shape=jax.ShapeDtypeStruct(hidden.sh...  76.5 us
    pallas_call x1, Pallas kernels, convolution(): pl.pallas_call(conv_kernel, out_shape=(jax.ShapeDtypeStruct((3, 208, chan...  54.9 us
    unnamed x11, local copies, waits for them, and re-layouts  5.83 us

profile of v2, /device:TPU:1, one launch (start us, length us, event | category | flops | bytes accessed | tf_op | source)
XLA Modules:
  0.0 139.3 jit_solution(8267323139528776042)
XLA Ops:
  0.0 0.7 reshape.12.bias
  0.7 0.7 reshape.13.gain
  1.4 0.7 reshape.14.gain
  2.0 0.0 copy-start
  2.1 1.6 %copy-done = bf16[2592,384]{1,0:T(8,128)(2,1)S(1)} copy-done((bf16[2592,384]{1,0:T(8,128)(2,1)S(1)}, bf16[2592,384]{1,0:T(8,128)(2,1)}, u32[]{:S(2)}) %copy-start) | copy-done | bytes 1990680
  3.6 0.0 copy-start.1
  3.6 1.0 copy-done.1
  4.6 0.0 copy-start.2
  4.6 0.9 copy-done.2
  5.6 0.0 copy-start.3
  5.6 0.9 copy-done.3
  6.5 0.0 copy-start.4
  6.5 0.7 copy-done.4
  7.1 54.9 %shard_map.82 = (bf16[3,208,384]{2,1,0:T(8,128)(2,1)S(1)}, bf16[384,1152]{1,0:T(8,128)(2,1)S(1)}, bf16[384,384]{1,0:T(8,128)(2,1)S(1)}) custom-call(bf16[1,3,2,104,384]{4,3,2,1,0:T(8,128)(2,1)S(1)} %copy-done.1, s32[1,3]{1,0:T(1,128)S(1)} %copy-done.4, bf16[2592,384]{1,0:T(8,128)(2,1)S(1)} %copy-done, bf16[96,1152]{1,0:T(8,128)(2,1)S(1)} %copy-done.2, ...), custom_call_target="tpu_custom_call" | custom-call | flops 4968677376 | bytes 7962624 | tf_op jit(solution)/shard_map/pallas_call | solution.py:546
  62.1 76.5 %shard_map.83 = bf16[3,208,384]{2,1,0:T(8,128)(2,1)S(1)} custom-call(bf16[3,208,384]{2,1,0:T(8,128)(2,1)S(1)} %get-tuple-element.8.hid, bf16[384,1152]{1,0:T(8,128)(2,1)S(1)} %get-tuple-element.9.qkv, bf16[384,384]{1,0:T(8,128)(2,1)S(1)} %get-tuple-element.10.outw, f32[1,384]{1,0:T(1,128)S(1)} %reshape.14.gain), custom_call_target="tpu_custom_call" | custom-call | flops 8506048512 | bytes 958464 | tf_op jit(solution)/shard_map/pallas_call | solution.py:240
  138.5 0.8 copy.10
Async XLA Ops:
  2.0 1.6 %copy-start = (bf16[2592,384]{1,0:T(8,128)(2,1)S(1)}, bf16[2592,384]{1,0:T(8,128)(2,1)}, u32[]{:S(2)}) copy-start(bf16[2592,384]{1,0:T(8,128)(2,1)} %w.1) | copy-start | bytes 5971972
  3.6 1.0 copy-start.1
  4.6 0.9 copy-start.2
  5.6 0.9 copy-start.3
  6.5 0.7 copy-start.4

commit v3 on v0

v3 whole, which is shorter than its diff:
```python
import math

import jax
import jax.numpy as jnp
from jax import lax
from jax.experimental import pallas as pl
from jax.experimental.pallas import tpu as pltpu
from jax.sharding import PartitionSpec as P

EPS = 1e-06
MESH = pl.DeviceIdType.MESH
BF = jnp.bfloat16
F32 = jnp.float32
XS = 4
ZS = 8
YS = 4
QUARTER = 2592
HALF = 1280
XPIECE = HALF // XS
ZPIECE = HALF // ZS
REST = 16
WIDE = 112
CHUNKS = ((0, 48), (48, 48), (96, 48), (144, 64))


def rms_scale(values, gain):
    values = values.astype(F32)
    return values * lax.rsqrt(jnp.mean(values * values, axis=-1, keepdims=True) + EPS) * gain


def dot(a, b):
    return jnp.dot(a, b, preferred_element_type=F32)


def dot_t(a, b):
    return lax.dot_general(a, b, (((1,), (1,)), ((), ())), preferred_element_type=F32)


def kernel(
    feat, fidx, w, qkvw, ow, bias, norm_gain, attn_gain, out,
    featv, wb, qkv, outw, u, lhs, acc, hid, nbuf, kb0, kb1, kb2, kb3, qbuf, mbuf, lbuf, mix, obuf, rbuf,
    local_sem, y_send, y_recv, ring_send, ring_on, ring_recv, s_send, s_recv, h_send, h_recv,
    home_send, home_recv, col_send, col_recv, pair_send, pair_recv, ret_send, ret_recv,
):
    chans = feat.shape[-1]
    width = feat.shape[-2]
    t = lax.axis_index("tm")
    space = lax.axis_index("space")
    y = lax.axis_index("dp")
    z, x = lax.div(space, XS), lax.rem(space, XS)
    left, right, across = lax.rem(x + XS - 1, XS), lax.rem(x + 1, XS), lax.rem(x + 2, XS)
    down, up = lax.rem(z + ZS - 1, ZS), lax.rem(z + 1, ZS)
    before, after = lax.rem(space + XS * ZS - 1, XS * ZS), lax.rem(space + 1, XS * ZS)
    parity = lax.rem(z, 2)
    slot = lax.div(z, 2)
    same = t == parity

    def dev(core, row, col):
        return {"tm": core, "space": row * XS + col}

    sib, lft, rgt = dev(1 - t, z, x), dev(t, z, left), dev(t, z, right)
    dwn, upw = dev(t, down, x), dev(t, up, x)

    def rows(start, count):
        return pl.ds(pl.multiple_of(start, 16), count)

    mine = (
        pltpu.make_async_copy(w, wb.at[rows(y * QUARTER, QUARTER)], local_sem.at[0]),
        pltpu.make_async_copy(qkvw, qkv.at[rows(y * 96, 96)], local_sem.at[1]),
        pltpu.make_async_copy(ow, outw.at[rows(y * 96, 96)], local_sem.at[2]),
    )
    fetch = pltpu.make_async_copy(feat.at[0], featv, local_sem.at[3])
    fetch.start()
    barrier = pltpu.get_barrier_semaphore()

    def greet(device):
        pl.semaphore_signal(barrier, inc=1, device_id=device, device_id_type=MESH)

    for d in range(1, YS):
        greet({"dp": lax.rem(y + d, YS)})
    for device in (sib, lft, rgt):
        greet(device)
    for core in range(2):
        for d in range(1, ZS):
            greet(dev(core, lax.rem(z + d, ZS), x))
    greet({"space": before})
    greet({"space": after})
    for c in mine:
        c.start()
    fetch.wait()

    pad = jnp.zeros((WIDE - width, chans), F32)
    for f in range(3):
        for r in range(2):
            scaled = rms_scale(featv[f, r], norm_gain[...])
            act = scaled * jax.nn.sigmoid(scaled)
            u[1 + r, 2 + f] = jnp.concatenate([act, pad], axis=0).astype(BF)
    blank = jnp.zeros((3, WIDE, chans), BF)

    @pl.when(space == 0)
    def _():
        u[0, 2:5] = blank
        u[0, 0:2] = blank[:2]

    @pl.when(space == XS * ZS - 1)
    def _():
        u[3, 2:5] = blank
        u[3, 0:2] = blank[:2]

    @pl.when(t == 0)
    def _():
        for r in range(4):
            u[r, 0:2] = blank[:2]

    pl.semaphore_wait(barrier, YS - 1 + 3 + 2 * (ZS - 1) + 2)

    def copy(src, dst, send, rec, device):
        return pltpu.make_async_remote_copy(
            src_ref=src, dst_ref=dst, send_sem=send, recv_sem=rec, device_id=device, device_id_type=MESH
        )

    def landed(ref, sem):
        copy(ref, ref, s_send.at[0, 0], sem, sib).wait_recv()

    owner = [lax.rem(y + d, YS) for d in (3, 1, 2)]
    target = [{"dp": lax.rem(y + d, YS)} for d in (1, 3, 2)]

    def rim(src, dst, n, device):
        return copy(src, dst, h_send.at[n], h_recv.at[n], device)

    has_after, has_before = space < XS * ZS - 1, space > 0
    rims = (
        (has_after, rim(u.at[2, 2:5], u.at[0, 2:5], 0, {"space": after})),
        (has_before, rim(u.at[1, 2:5], u.at[3, 2:5], 1, {"space": before})),
    )
    prior = (
        (t == 0, rim(u.at[1:3, 3:5], u.at[1:3, 0:2], 2, sib)),
        (jnp.logical_and(t == 0, has_before), rim(u.at[0, 3:5], u.at[0, 0:2], 3, sib)),
        (jnp.logical_and(t == 0, has_after), rim(u.at[3, 3:5], u.at[3, 0:2], 4, sib)),
    )

    def send_rims():
        for cond, c in rims:
            pl.when(cond)(c.start)
        pl.when(t == 0)(prior[0][1].start)

    def take_rims():
        pl.when(has_before)(rims[0][1].wait_recv)
        pl.when(has_after)(rims[1][1].wait_recv)
        for cond, c in prior[1:]:
            pl.when(cond)(c.start)

    def take_prior():
        for cond, (_, c) in zip(
            (t == 1, jnp.logical_and(t == 1, has_before), jnp.logical_and(t == 1, has_after)), prior
        ):
            pl.when(cond)(c.wait_recv)

    keep = [[(fidx[0, f] >= 2 - kt).astype(F32) for f in range(3)] for kt in range(2)]

    def spread(g, r):
        cells = u[r, g].astype(F32)
        for kw in range(3):
            moved = cells if kw == 1 else pltpu.roll(cells, 1 if kw == 0 else WIDE - 1, 0)
            for kt in range(3):
                f = g - kt
                if 0 <= f < 3:
                    lhs[kt * 3 + kw, f, r] = (moved if kt == 2 else moved * keep[kt][f]).astype(BF)

    def spread_own():
        for g in range(2, 5):
            for r in range(1, 3):
                spread(g, r)

    def spread_rims():
        for g in range(2, 5):
            spread(g, 0)
            spread(g, 3)

    def spread_prior():
        for g in range(2):
            for r in range(4):
                spread(g, r)

    def tap(number):
        if isinstance(number, int):
            kt, kh, kw = number // 9, (number // 3) % 3, number % 3
        else:
            kt, kh, kw = lax.div(number, 9), lax.rem(lax.div(number, 3), 3), lax.rem(number, 3)
        cells = lhs[kt * 3 + kw, :, pl.ds(kh, 2)].reshape(-1, chans)
        acc[...] += dot(cells, wb[rows(number * chans, chans)])

    def taps(j, first, last):
        @pl.loop(first, last)
        def _(i):
            tap(7 * j + i)

    def half_rows(j, core):
        return rows(j * QUARTER + core * HALF, HALF)

    def rest_rows(j, core):
        return rows(j * QUARTER + 2 * HALF + core * REST, REST)

    def proj_rows(j, core):
        return rows(j * 96 + core * 48, 48)

    def small_refs(j, core):
        return wb.at[rest_rows(j, core)], qkv.at[proj_rows(j, core)], outw.at[proj_rows(j, core)]

    def ring_core(core):
        sent = []

        def go(c):
            c.start()
            sent.append(c)

        def push(ref, send, rec, device):
            go(copy(ref, ref, send, rec, device))

        def piece(j, n, part=0, parts=1):
            size = XPIECE if core == 0 else ZPIECE
            return wb.at[rows(j * QUARTER + core * HALF + n * size + part * (size // parts), size // parts)]

        place = x if core == 0 else z
        size = XPIECE if core == 0 else ZPIECE
        ahead, behind = (rgt, lft) if core == 0 else (upw, dwn)

        def to_y(k):
            src = w.at[rows(core * HALF + place * size, size)]
            go(copy(src, piece(y, place), y_send.at[k, 0], y_recv.at[k, 0], target[k]))

        def to_y_small(k):
            srcs = w.at[rows(2 * HALF + core * REST, REST)], qkvw.at[rows(core * 48, 48)], ow.at[rows(core * 48, 48)]
            for n, (src, dst) in enumerate(zip(srcs, small_refs(y, core))):
                go(copy(src, dst, y_send.at[k, 1 + n], y_recv.at[k, 1 + n], target[k]))

        def from_y(k):
            ref = piece(owner[k], place)
            landed(ref, y_recv.at[k, 0])
            push(ref, ring_send.at[k, 0], ring_recv.at[k, 0], ahead)
            push(ref, ring_send.at[k, 1], ring_recv.at[k, 1], behind)

        def small(k):
            for n, ref in enumerate(small_refs(owner[k], core)):
                landed(ref, y_recv.at[k, 1 + n])
                push(ref, s_send.at[k, 1 + n], s_recv.at[k, 1 + n], sib)

        count = XS if core == 0 else ZS
        last = count // 2

        def step(k, d):
            for way, on in enumerate((ahead, behind)):
                n = lax.rem(place + (count - d if way == 0 else d), count)
                landed(piece(owner[k], n), ring_recv.at[k, 2 * d - 2 + way])
                ref = piece(owner[k], n)
                if d == last - 1:
                    ref = piece(owner[k], n, way, 2)
                push(ref, ring_on.at[k, 2 * d - 2 + way], ring_recv.at[k, 2 * d + way], on)

        def end(k):
            n = lax.rem(place + last, count)
            for way in range(2):
                landed(piece(owner[k], n, way, 2), ring_recv.at[k, 2 * last - 2 + way])
            push(wb.at[half_rows(owner[k], core)], s_send.at[k, 0], s_recv.at[k, 0], sib)

        def shared(k):
            landed(wb.at[half_rows(owner[k], 1 - core)], s_recv.at[k, 0])
            landed(wb.at[rest_rows(owner[k], 1 - core)], s_recv.at[k, 1])

        to_y(0)
        to_y(1)
        send_rims()
        acc[...] = jnp.zeros_like(acc)
        spread_own()
        from_y(0)
        from_y(1)
        to_y(2)
        for k in range(3):
            to_y_small(k)
        take_rims()
        if core == 0:
            spread_rims()
            step(0, 1)
            step(1, 1)
            from_y(2)
            take_prior()
            spread_prior()
            end(0)
            end(1)
            step(2, 1)
            mine[0].wait()
            taps(y, 0, 4)
            end(2)
            taps(y, 4, 6)
            for k in range(3):
                small(k)
        else:
            step(0, 1)
            step(1, 1)
            spread_rims()
            from_y(2)
            step(0, 2)
            step(1, 2)
            take_prior()
            spread_prior()
            step(0, 3)
            step(1, 3)
            step(2, 1)
            mine[0].wait()
            taps(y, 0, 3)
            end(0)
            end(1)
            step(2, 2)
            for k in range(3):
                small(k)
            taps(y, 3, 6)
            step(2, 3)
        shared(0)
        if core == 0:
            taps(owner[0], 0, 6)
        else:
            taps(owner[0], 0, 4)
            end(2)
            taps(owner[0], 4, 6)
        shared(1)
        taps(owner[1], 0, 6)
        shared(2)
        taps(owner[2], 0, 6)
        for c in sent:
            c.wait_send()

    for core in range(2):
        @pl.when(t == core)
        def _():
            ring_core(core)

    for number in (6, 13, 20):
        tap(number)

    for f in range(3):
        both = []
        for r in range(2):
            part = acc[pl.ds((f * 2 + r) * WIDE, width)]
            both.append(featv[f, r].astype(F32) + part + bias[...])
        hid[f] = jnp.concatenate(both, axis=0).astype(BF)
        nbuf[f] = rms_scale(hid[f], attn_gain[...]).astype(BF)

    kbs = (kb0, kb1, kb2, kb3)

    def home_copy(c, j):
        first, count = CHUNKS[c]
        dst = kbs[c].at[x, parity, slot]
        return copy(
            nbuf.at[j, pl.ds(first, count)], dst, home_send.at[c, j], home_recv.at[c, slot], dev(parity, 2 * j + t, x)
        )

    for c in range(4):
        for j in range(3):
            pl.when(2 * j + t != z)(home_copy(c, j).start)

    for k in range(3):
        landed(qkv.at[proj_rows(owner[k], 1 - t)], s_recv.at[k, 2])
        landed(outw.at[proj_rows(owner[k], 1 - t)], s_recv.at[k, 3])
    mine[1].wait()
    mine[2].wait()

    is_worker = z < 6

    @pl.when(is_worker)
    def _():
        sent = []

        def push(ref, send, rec, device):
            c = copy(ref, ref, send, rec, device)
            c.start()
            sent.append(c)

        def own(c):
            first, count = CHUNKS[c]

            @pl.when(same)
            def _():
                kbs[c][x, t, slot] = nbuf[slot, pl.ds(first, count)]

            for h in range(4):
                @pl.when(jnp.logical_not(jnp.logical_and(same, slot == h)))
                def _():
                    landed(kbs[c].at[x, t, h], home_recv.at[c, h])

            ref = kbs[c].at[x, t]
            push(ref, col_send.at[c, 0], col_recv.at[c, 0], rgt)
            push(ref, col_send.at[c, 1], col_recv.at[c, 1], lft)
            push(ref, pair_send.at[c, 0], pair_recv.at[c, 0], sib)

        def beside(c):
            for way, (col, on) in enumerate(((left, rgt), (right, lft))):
                ref = kbs[c].at[col, t]
                landed(ref, col_recv.at[c, way])
                push(kbs[c].at[col, t, pl.ds(2 * way, 2)], col_send.at[c, 2 + way], col_recv.at[c, 2 + way], on)
                push(ref, pair_send.at[c, 1 + way], pair_recv.at[c, 1 + way], sib)

        def far(c):
            for way in range(2):
                landed(kbs[c].at[across, t, pl.ds(2 * way, 2)], col_recv.at[c, 2 + way])
            push(kbs[c].at[across, t], pair_send.at[c, 3], pair_recv.at[c, 3], sib)

        def others(c):
            for n, col in enumerate((x, left, right, across)):
                landed(kbs[c].at[col, 1 - t], pair_recv.at[c, n])

        def project(c):
            first, count = CHUNKS[c]
            n = kbs[c][x, t].reshape(-1, chans)
            q = dot(n, qkv[:, :chans]).astype(BF)
            qk = dot_t(q, qkv[:, chans : 2 * chans]) * (math.log2(math.e) / math.sqrt(chans))
            qbuf[:, pl.ds(first, count)] = qk.astype(BF).reshape(4, count, chans)

        def attend(i, c):
            keys = kbs[c][...].reshape(-1, chans)
            s = dot_t(qbuf[i], keys)
            top = jnp.max(s, axis=-1, keepdims=True)
            if c > 0:
                top = jnp.maximum(top, mbuf[i])
            p = jnp.exp2(s - top)
            total = jnp.sum(p, axis=-1, keepdims=True)
            mixed = dot(p.astype(BF), keys)
            if c > 0:
                alpha = jnp.exp2(mbuf[i] - top)
                total = total + lbuf[i] * alpha
                mixed = mixed + mix[i] * alpha
            mbuf[i] = top
            lbuf[i] = total
            mix[i] = mixed

        def back(i):
            return copy(obuf.at[i], rbuf.at[slot], ret_send.at[i], ret_recv.at[slot], dev(parity, 2 * i + t, x))

        def finish(i):
            mixed = (mix[i] * (1.0 / lbuf[i])).astype(BF)
            attended = dot(mixed, qkv[:, 2 * chans :]).astype(BF)
            at_home = jnp.logical_and(same, slot == i)

            @pl.when(at_home)
            def _():
                rbuf[slot] = attended

            @pl.when(jnp.logical_not(at_home))
            def _():
                obuf[i] = attended
                back(i).start()

        own(0)
        project(0)
        own(1)
        project(1)
        beside(0)
        own(2)
        project(2)
        beside(1)
        far(0)
        own(3)
        project(3)
        others(0)
        attend(0, 0)
        beside(2)
        attend(1, 0)
        far(1)
        attend(2, 0)
        attend(3, 0)
        others(1)
        attend(0, 1)
        beside(3)
        attend(1, 1)
        far(2)
        attend(2, 1)
        attend(3, 1)
        others(2)
        attend(0, 2)
        attend(1, 2)
        far(3)
        attend(2, 2)
        attend(3, 2)
        others(3)

        @pl.loop(0, 4)
        def _(n):
            i = lax.rem(slot + 2 + jnp.where(n == 1, 3, jnp.where(n == 2, 1, n * 2)), 4)
            attend(i, 3)
            finish(i)

        for c in sent:
            c.wait_send()
        for i in range(4):
            pl.when(jnp.logical_not(jnp.logical_and(same, slot == i)))(back(i).wait_send)

    for j in range(3):
        @pl.when(2 * j + t != z)
        def _():
            for c in range(4):
                home_copy(c, j).wait_send()
            landed(rbuf.at[j], ret_recv.at[j])

        result = hid[j].astype(F32) + dot(rbuf[j], outw[...])
        for r in range(2):
            out[0, j, r] = result[r * width : (r + 1) * width].astype(BF)

    for cond, c in rims + prior:
        pl.when(cond)(c.wait_send)


def on_device(
    features, frame_index, conv_weight, conv_bias, norm_gain, attn_gain, qkv_weight, out_weight
):
    frames, height, width, chans = features.shape[1:]
    pixels = height * width
    vmem = pl.BlockSpec(memory_space=pltpu.VMEM)
    smem = pl.BlockSpec(memory_space=pltpu.SMEM)
    hbm = pl.BlockSpec(memory_space=pltpu.HBM)
    dma = pltpu.SemaphoreType.DMA
    blocks = [pltpu.VMEM((XS, 2, 4, count, chans), BF) for _, count in CHUNKS]
    return pl.pallas_call(
        kernel,
        out_shape=jax.ShapeDtypeStruct(features.shape, BF),
        in_specs=[hbm, smem, hbm, hbm, hbm, vmem, vmem, vmem],
        out_specs=vmem,
        scratch_shapes=[
            pltpu.VMEM((frames, height, width, chans), BF),
            pltpu.VMEM((YS * QUARTER, chans), BF),
            pltpu.VMEM((chans, 3 * chans), BF),
            pltpu.VMEM((chans, chans), BF),
            pltpu.VMEM((4, 5, WIDE, chans), BF),
            pltpu.VMEM((9, 3, 4, WIDE, chans), BF),
            pltpu.VMEM((6 * WIDE, chans), F32),
            pltpu.VMEM((frames, pixels, chans), BF),
            pltpu.VMEM((frames, pixels, chans), BF),
            *blocks,
            pltpu.VMEM((4, pixels, chans), BF),
            pltpu.VMEM((4, pixels, 1), F32),
            pltpu.VMEM((4, pixels, 1), F32),
            pltpu.VMEM((4, pixels, chans), F32),
            pltpu.VMEM((4, pixels, chans), BF),
            pltpu.VMEM((3, pixels, chans), BF),
            dma((4,)), dma((3, 4)), dma((3, 4)), dma((3, 2)), dma((3, 6)), dma((3, 8)),
            dma((3, 4)), dma((3, 4)), dma((5,)), dma((5,)),
            dma((4, 3)), dma((4, 4)), dma((4, 4)), dma((4, 4)), dma((4, 4)), dma((4, 4)), dma((4,)), dma((3,)),
        ],
        compiler_params=pltpu.CompilerParams(
            collective_id=1, has_side_effects=True, vmem_limit_bytes=60 * 1024 * 1024
        ),
        cost_estimate=pl.CostEstimate(
            flops=2 * frames * pixels * chans * chans * 31 + 4 * 4 * pixels * 32 * pixels * chans,
            bytes_accessed=4 * frames * pixels * chans + 2 * QUARTER * chans,
            transcendentals=4 * pixels * 32 * pixels,
        ),
    )(features, frame_index, conv_weight, qkv_weight, out_weight, conv_bias, norm_gain, attn_gain)


def solution(mesh):
    placed = (
        P("dp", "tm", "space", None, None),
        P("dp", "tm"),
        P("dp", None),
        P(),
        P(),
        P(),
        P("dp", None),
        P("dp", None),
    )
    return jax.shard_map(
        on_device,
        mesh=mesh,
        in_specs=placed,
        out_specs=P("dp", "tm", "space", None, None),
        check_vma=False,
    )
```

time: 386 us -> 111 us (0.29)
  waiting for transfers between devices: 247 us -> 0 us
  Pallas kernels: 0 us -> 109 us
  matrix products: 40.2 us -> 0 us
  blocking collectives: 28.3 us -> 0 us
  other arithmetic: 27.7 us -> 0 us
  local copies, waits for them, and re-layouts: 22.7 us -> 1.85 us
  between operations: 13.5 us -> 0.01 us
  starting transfers between devices: 6.58 us -> 0 us
    all_gather x2 -> x0, waiting for transfers between devices: 240 us -> none  [the longest x1 207 us: on_device(): frame_pairs = lax.all_gather(local_pairs, 'space', axis=1, tiled=True)]
    pallas_call x0 -> x1, Pallas kernels: none -> 109 us  [on_device(): pl.pallas_call(kernel, out_shape=jax.ShapeDtypeStruct(features.shape, BF)...]
    dot_general x6 -> x0, matrix products: 40.2 us -> none  [the longest x1 13.4 us: on_device(): jnp.einsum('fqk,fkc->fqc', probs, values, preferred_element_type=jnp.floa...]
    all_gather x2 -> x0, blocking collectives: 28.3 us -> none  [the longest x1 18.2 us: on_device(): lax.all_gather(qkv_weight, 'dp', axis=0, tiled=True)]
    sub x1 -> x0, other arithmetic: 20.7 us -> none  [on_device(): shifted = jnp.exp(scores - jnp.max(scores, axis=-1, keepdims=True))]
    unnamed x33 -> x1, local copies, waits for them, and re-layouts: 21.2 us -> 1.85 us
    ppermute x3 -> x0, waiting for transfers between devices: 6.97 us -> none  [the longest x1 3.81 us: with_halo(): lax.ppermute(head, axis, [((i + 1) % count, i) for i in range(ends)])]
    ppermute x3 -> x0, starting transfers between devices: 6.54 us -> none  [the longest x1 3.96 us: with_halo(): lax.ppermute(tail, axis, [(i, (i + 1) % count) for i in range(ends)])]
  transfers between devices with their start and end apart: 5 -> 0, of which waited for: 4 -> 0; matrix products, arithmetic and copies ran while one was open for 8% -> 0% of each run, Pallas kernels for 0% -> 0%
where the time goes in v3:
time: 111 us
  Pallas kernels  109 us (98%)
  local copies, waits for them, and re-layouts  1.85 us (2%)
    pallas_call x1, Pallas kernels, on_device(): pl.pallas_call(kernel, out_shape=jax.ShapeDtypeStruct(features.shape, BF)...  109 us

profile of v3, /device:TPU:1, one launch (start us, length us, event | category | flops | bytes accessed | tf_op | source)
XLA Modules:
  0.0 111.1 jit_solution(15730317274187913618)
XLA Ops:
  0.0 109.2 %shard_map.82 = bf16[1,3,2,104,384]{4,3,2,1,0:T(8,128)(2,1)} custom-call(bf16[1,3,2,104,384]{4,3,2,1,0:T(8,128)(2,1)} %feat.1, s32[1,3]{1,0:T(1,128)} %fidx.1, bf16[2592,384]{1,0:T(8,128)(2,1)} %w.1, bf16[96,1152]{1,0:T(8,128)(2,1)} %qkvw.1, bf16[96,384]{1,0:T(8,128)(2,1)} %ow.1, f32[384]{0:T(512)} %bias.1, f32[384]{0:T(512)} %norm_gain.1, f32[384]{0:T(512)} %attn_gain.1), custom_call_target="tpu_custom_call" | custom-call | flops 14210826240 | bytes 2949120 | tf_op jit(solution)/shard_map/pallas_call | solution.py:521
  109.3 1.8 %copy.10 = bf16[1,3,2,104,384]{4,3,2,1,0:T(8,128)(2,1)} copy(bf16[1,3,2,104,384]{4,3,2,1,0:T(8,128)(2,1)} %shard_map.82) | data formatting | bytes 958464

commit v4 on v3

--- a/solution.py
+++ b/solution.py
@@ -15,10 +15,11 @@
 ZS = 8
 YS = 4
 QUARTER = 2592
-HALF = 1280
-XPIECE = HALF // XS
-ZPIECE = HALF // ZS
-REST = 16
+XPART = 1152
+ZPART = 896
+REST = 272
+XPIECE = XPART // XS
+ZPIECE = ZPART // ZS
 WIDE = 112
 CHUNKS = ((0, 48), (48, 48), (96, 48), (144, 64))
 
@@ -38,8 +39,8 @@
 
 def kernel(
     feat, fidx, w, qkvw, ow, bias, norm_gain, attn_gain, out,
-    featv, wb, qkv, outw, u, lhs, acc, hid, nbuf, kb0, kb1, kb2, kb3, qbuf, mbuf, lbuf, mix, obuf, rbuf,
-    local_sem, y_send, y_recv, ring_send, ring_on, ring_recv, s_send, s_recv, h_send, h_recv,
+    featv, wb, qkv, outw, u, lhs, acc, hid, nbuf, kb0, kb1, kb2, kb3, q0, q1, m0, m1, l0, l1, mix0, mix1, obuf, rbuf,
+    local_sem, y_send, y_recv, ring_send, ring_on, ring_recv, s_send, s_recv, p_send, p_recv, h_send, h_recv,
     home_send, home_recv, col_send, col_recv, pair_send, pair_recv, ret_send, ret_recv,
 ):
     chans = feat.shape[-1]
@@ -60,6 +61,7 @@
 
     sib, lft, rgt = dev(1 - t, z, x), dev(t, z, left), dev(t, z, right)
     dwn, upw = dev(t, down, x), dev(t, up, x)
+    dwn2, upw2 = dev(t, lax.rem(z + ZS - 2, ZS), x), dev(t, lax.rem(z + 2, ZS), x)
 
     def rows(start, count):
         return pl.ds(pl.multiple_of(start, 16), count)
@@ -87,14 +89,7 @@
     greet({"space": after})
     for c in mine:
         c.start()
-    fetch.wait()
-
-    pad = jnp.zeros((WIDE - width, chans), F32)
-    for f in range(3):
-        for r in range(2):
-            scaled = rms_scale(featv[f, r], norm_gain[...])
-            act = scaled * jax.nn.sigmoid(scaled)
-            u[1 + r, 2 + f] = jnp.concatenate([act, pad], axis=0).astype(BF)
+
     blank = jnp.zeros((3, WIDE, chans), BF)
 
     @pl.when(space == 0)
@@ -113,6 +108,15 @@
             u[r, 0:2] = blank[:2]
 
     pl.semaphore_wait(barrier, YS - 1 + 3 + 2 * (ZS - 1) + 2)
+
+    def activate():
+        fetch.wait()
+        pad = jnp.zeros((WIDE - width, chans), F32)
+        for f in range(3):
+            for r in range(2):
+                scaled = rms_scale(featv[f, r], norm_gain[...])
+                act = scaled * jax.nn.sigmoid(scaled)
+                u[1 + r, 2 + f] = jnp.concatenate([act, pad], axis=0).astype(BF)
 
     def copy(src, dst, send, rec, device):
         return pltpu.make_async_remote_copy(
@@ -182,160 +186,162 @@
             for r in range(4):
                 spread(g, r)
 
-    def tap(number):
+    def window(number):
         if isinstance(number, int):
             kt, kh, kw = number // 9, (number // 3) % 3, number % 3
         else:
             kt, kh, kw = lax.div(number, 9), lax.rem(lax.div(number, 3), 3), lax.rem(number, 3)
-        cells = lhs[kt * 3 + kw, :, pl.ds(kh, 2)].reshape(-1, chans)
-        acc[...] += dot(cells, wb[rows(number * chans, chans)])
-
-    def taps(j, first, last):
-        @pl.loop(first, last)
-        def _(i):
-            tap(7 * j + i)
-
-    def half_rows(j, core):
-        return rows(j * QUARTER + core * HALF, HALF)
+        return lhs[kt * 3 + kw, :, pl.ds(kh, 2)].reshape(-1, chans)
+
+    def three_taps(j, half):
+        first = 7 * j + 3 * half
+        cells = jnp.concatenate([window(first + n) for n in range(3)], axis=1)
+        acc[...] += dot(cells, wb[rows(first * chans, 3 * chans)])
+
+    def six_taps(j):
+        three_taps(j, 0)
+        three_taps(j, 1)
 
     def rest_rows(j, core):
-        return rows(j * QUARTER + 2 * HALF + core * REST, REST)
-
-    def proj_rows(j, core):
-        return rows(j * 96 + core * 48, 48)
+        return rows(j * QUARTER + XPART + ZPART + core * REST, REST)
+
+    sent = [], []
 
     def small_refs(j, core):
-        return wb.at[rest_rows(j, core)], qkv.at[proj_rows(j, core)], outw.at[proj_rows(j, core)]
+        part = rows(j * 96 + core * 48, 48)
+        return qkv.at[part], outw.at[part]
+
+    def small_copies(k):
+        part = rows(t * 48, 48)
+        return [
+            copy(src, dst, y_send.at[k, 2 + n], y_recv.at[k, 2 + n], target[k])
+            for n, (src, dst) in enumerate(zip((qkvw.at[part], ow.at[part]), small_refs(y, t)))
+        ]
+
+    def small_shares(k):
+        return [copy(ref, ref, p_send.at[k, n], p_recv.at[k, n], sib) for n, ref in enumerate(small_refs(owner[k], t))]
 
     def ring_core(core):
-        sent = []
-
-        def go(c):
-            c.start()
-            sent.append(c)
-
-        def push(ref, send, rec, device):
-            go(copy(ref, ref, send, rec, device))
+        def go(src, dst, count, send, rec, device):
+            copy(src, dst, send[0].at[send[1], send[2]], rec, device).start()
+            sent[core].append((count, send))
+
+        size = XPIECE if core == 0 else ZPIECE
+        place = x if core == 0 else z
 
         def piece(j, n, part=0, parts=1):
-            size = XPIECE if core == 0 else ZPIECE
-            return wb.at[rows(j * QUARTER + core * HALF + n * size + part * (size // parts), size // parts)]
-
-        place = x if core == 0 else z
-        size = XPIECE if core == 0 else ZPIECE
-        ahead, behind = (rgt, lft) if core == 0 else (upw, dwn)
+            start = j * QUARTER + core * XPART + n * size + part * (size // parts)
+            return wb.at[rows(start, size // parts)]
 
         def to_y(k):
-            src = w.at[rows(core * HALF + place * size, size)]
-            go(copy(src, piece(y, place), y_send.at[k, 0], y_recv.at[k, 0], target[k]))
-
-        def to_y_small(k):
-            srcs = w.at[rows(2 * HALF + core * REST, REST)], qkvw.at[rows(core * 48, 48)], ow.at[rows(core * 48, 48)]
-            for n, (src, dst) in enumerate(zip(srcs, small_refs(y, core))):
-                go(copy(src, dst, y_send.at[k, 1 + n], y_recv.at[k, 1 + n], target[k]))
+            src = w.at[rows(core * XPART + place * size, size)]
+            go(src, piece(y, place), size, (y_send, k, 0), y_recv.at[k, 0], target[k])
+
+        def to_y_rest(k):
+            src = w.at[rows(XPART + ZPART + core * REST, REST)]
+            go(src, wb.at[rest_rows(y, core)], REST, (y_send, k, 1), y_recv.at[k, 1], target[k])
+
+        def push(ref, send, rec, device, count=size):
+            go(ref, ref, count, send, rec, device)
+
+        def share(k, n, ref):
+            push(ref, (s_send, k, n), s_recv.at[k, n], sib)
+
+        def rest(k):
+            ref = wb.at[rest_rows(owner[k], core)]
+            landed(ref, y_recv.at[k, 1])
+            push(ref, (s_send, k, 8), s_recv.at[k, 8], sib, REST)
 
         def from_y(k):
             ref = piece(owner[k], place)
             landed(ref, y_recv.at[k, 0])
-            push(ref, ring_send.at[k, 0], ring_recv.at[k, 0], ahead)
-            push(ref, ring_send.at[k, 1], ring_recv.at[k, 1], behind)
-
-        def small(k):
-            for n, ref in enumerate(small_refs(owner[k], core)):
-                landed(ref, y_recv.at[k, 1 + n])
-                push(ref, s_send.at[k, 1 + n], s_recv.at[k, 1 + n], sib)
-
-        count = XS if core == 0 else ZS
-        last = count // 2
-
-        def step(k, d):
-            for way, on in enumerate((ahead, behind)):
-                n = lax.rem(place + (count - d if way == 0 else d), count)
-                landed(piece(owner[k], n), ring_recv.at[k, 2 * d - 2 + way])
+            for n, on in enumerate((rgt, lft) if core == 0 else (upw, dwn, upw2, dwn2)):
+                push(ref, (ring_send, k, n), ring_recv.at[k, n], on)
+            share(k, 0, ref)
+
+        def x_on(k):
+            for way, (n, on) in enumerate(((left, rgt), (right, lft))):
                 ref = piece(owner[k], n)
-                if d == last - 1:
-                    ref = piece(owner[k], n, way, 2)
-                push(ref, ring_on.at[k, 2 * d - 2 + way], ring_recv.at[k, 2 * d + way], on)
+                landed(ref, ring_recv.at[k, way])
+                half = piece(owner[k], n, way, 2)
+                push(half, (ring_on, k, way), ring_recv.at[k, 2 + way], on, size // 2)
+                share(k, 1 + way, ref)
+
+        def z_on(k):
+            for way, far in enumerate((ZS - 1, 1)):
+                ref = piece(owner[k], lax.rem(z + far, ZS))
+                landed(ref, ring_recv.at[k, way])
+                share(k, 1 + way, ref)
+            for way, (far, one, two) in enumerate(((ZS - 2, upw, upw2), (2, dwn, dwn2))):
+                ref = piece(owner[k], lax.rem(z + far, ZS))
+                landed(ref, ring_recv.at[k, 2 + way])
+                push(ref, (ring_on, k, way), ring_recv.at[k, 4 + way], one)
+                if way == k % 2:
+                    push(ref, (ring_on, k, 2), ring_recv.at[k, 6], two)
+                share(k, 3 + way, ref)
 
         def end(k):
-            n = lax.rem(place + last, count)
-            for way in range(2):
-                landed(piece(owner[k], n, way, 2), ring_recv.at[k, 2 * last - 2 + way])
-            push(wb.at[half_rows(owner[k], core)], s_send.at[k, 0], s_recv.at[k, 0], sib)
+            if core == 0:
+                for way in range(2):
+                    landed(piece(owner[k], across, way, 2), ring_recv.at[k, 2 + way])
+                share(k, 3, piece(owner[k], across))
+            else:
+                for n, far in ((4, ZS - 3), (5, 3), (6, 4)):
+                    ref = piece(owner[k], lax.rem(z + far, ZS))
+                    landed(ref, ring_recv.at[k, n])
+                    share(k, n + 1, ref)
 
         def shared(k):
-            landed(wb.at[half_rows(owner[k], 1 - core)], s_recv.at[k, 0])
-            landed(wb.at[rest_rows(owner[k], 1 - core)], s_recv.at[k, 1])
-
-        to_y(0)
-        to_y(1)
+            start = owner[k] * QUARTER
+            if core == 0:
+                for n, far in enumerate((0, ZS - 1, 1, ZS - 2, 2, ZS - 3, 3, 4)):
+                    first = start + XPART + lax.rem(z + far, ZS) * ZPIECE
+                    landed(wb.at[rows(first, ZPIECE)], s_recv.at[k, n])
+            else:
+                for n, col in enumerate((x, left, right, across)):
+                    landed(wb.at[rows(start + col * XPIECE, XPIECE)], s_recv.at[k, n])
+            landed(wb.at[rest_rows(owner[k], 1 - core)], s_recv.at[k, 8])
+
+        on = x_on if core == 0 else z_on
+        for k in range(3):
+            to_y(k)
+        for k in range(3):
+            to_y_rest(k)
+        for k in range(3):
+            for c in small_copies(k):
+                c.start()
+        activate()
         send_rims()
         acc[...] = jnp.zeros_like(acc)
         spread_own()
-        from_y(0)
-        from_y(1)
-        to_y(2)
         for k in range(3):
-            to_y_small(k)
+            from_y(k)
+        on(0)
         take_rims()
-        if core == 0:
-            spread_rims()
-            step(0, 1)
-            step(1, 1)
-            from_y(2)
-            take_prior()
-            spread_prior()
-            end(0)
-            end(1)
-            step(2, 1)
-            mine[0].wait()
-            taps(y, 0, 4)
-            end(2)
-            taps(y, 4, 6)
-            for k in range(3):
-                small(k)
-        else:
-            step(0, 1)
-            step(1, 1)
-            spread_rims()
-            from_y(2)
-            step(0, 2)
-            step(1, 2)
-            take_prior()
-            spread_prior()
-            step(0, 3)
-            step(1, 3)
-            step(2, 1)
-            mine[0].wait()
-            taps(y, 0, 3)
-            end(0)
-            end(1)
-            step(2, 2)
-            for k in range(3):
-                small(k)
-            taps(y, 3, 6)
-            step(2, 3)
-        shared(0)
-        if core == 0:
-            taps(owner[0], 0, 6)
-        else:
-            taps(owner[0], 0, 4)
-            end(2)
-            taps(owner[0], 4, 6)
-        shared(1)
-        taps(owner[1], 0, 6)
-        shared(2)
-        taps(owner[2], 0, 6)
-        for c in sent:
-            c.wait_send()
+        spread_rims()
+        on(1)
+        take_prior()
+        spread_prior()
+        on(2)
+        mine[0].wait()
+        end(0)
+        three_taps(y, 0)
+        rest(0)
+        end(1)
+        rest(1)
+        end(2)
+        rest(2)
+        three_taps(y, 1)
+        for k in range(3):
+            shared(k)
+            six_taps(owner[k])
 
     for core in range(2):
         @pl.when(t == core)
         def _():
             ring_core(core)
 
-    for number in (6, 13, 20):
-        tap(number)
+    acc[...] += sum(dot(window(n), wb[rows(n * chans, chans)]) for n in (6, 13, 20))
 
     for f in range(3):
         both = []
@@ -346,6 +352,7 @@
         nbuf[f] = rms_scale(hid[f], attn_gain[...]).astype(BF)
 
     kbs = (kb0, kb1, kb2, kb3)
+    groups = (q0, m0, l0, mix0), (q1, m1, l1, mix1)
 
     def home_copy(c, j):
         first, count = CHUNKS[c]
@@ -359,8 +366,13 @@
             pl.when(2 * j + t != z)(home_copy(c, j).start)
 
     for k in range(3):
-        landed(qkv.at[proj_rows(owner[k], 1 - t)], s_recv.at[k, 2])
-        landed(outw.at[proj_rows(owner[k], 1 - t)], s_recv.at[k, 3])
+        for n, ref in enumerate(small_refs(owner[k], t)):
+            landed(ref, y_recv.at[k, 2 + n])
+        for c in small_shares(k):
+            c.start()
+    for k in range(3):
+        for n, ref in enumerate(small_refs(owner[k], 1 - t)):
+            landed(ref, p_recv.at[k, n])
     mine[1].wait()
     mine[2].wait()
 
@@ -409,45 +421,54 @@
                 landed(kbs[c].at[col, 1 - t], pair_recv.at[c, n])
 
         def project(c):
-            first, count = CHUNKS[c]
+            count = CHUNKS[c][1]
             n = kbs[c][x, t].reshape(-1, chans)
             q = dot(n, qkv[:, :chans]).astype(BF)
             qk = dot_t(q, qkv[:, chans : 2 * chans]) * (math.log2(math.e) / math.sqrt(chans))
-            qbuf[:, pl.ds(first, count)] = qk.astype(BF).reshape(4, count, chans)
-
-        def attend(i, c):
+            groups[c // 2][0][pl.ds(0 if c % 2 == 0 else 4 * CHUNKS[c - 1][1], 4 * count)] = qk.astype(BF)
+
+        def attend(group, c):
+            queries, maxima, sums, mix = groups[group]
             keys = kbs[c][...].reshape(-1, chans)
-            s = dot_t(qbuf[i], keys)
+            s = dot_t(queries[...], keys)
             top = jnp.max(s, axis=-1, keepdims=True)
             if c > 0:
-                top = jnp.maximum(top, mbuf[i])
+                top = jnp.maximum(top, maxima[...])
             p = jnp.exp2(s - top)
             total = jnp.sum(p, axis=-1, keepdims=True)
             mixed = dot(p.astype(BF), keys)
             if c > 0:
-                alpha = jnp.exp2(mbuf[i] - top)
-                total = total + lbuf[i] * alpha
-                mixed = mixed + mix[i] * alpha
-            mbuf[i] = top
-            lbuf[i] = total
-            mix[i] = mixed
-
-        def back(i):
-            return copy(obuf.at[i], rbuf.at[slot], ret_send.at[i], ret_recv.at[slot], dev(parity, 2 * i + t, x))
-
-        def finish(i):
-            mixed = (mix[i] * (1.0 / lbuf[i])).astype(BF)
+                alpha = jnp.exp2(maxima[...] - top)
+                total = total + sums[...] * alpha
+                mixed = mixed + mix[...] * alpha
+            maxima[...] = top
+            sums[...] = total
+            mix[...] = mixed
+
+        def back(group, i):
+            first, count = CHUNKS[2 * group][0], CHUNKS[2 * group][1] + CHUNKS[2 * group + 1][1]
+            part = pl.ds(first, count)
+            return copy(
+                obuf.at[i, part], rbuf.at[slot, part], ret_send.at[group, i], ret_recv.at[slot, group],
+                dev(parity, 2 * i + t, x),
+            )
+
+        def finish(group):
+            _, _, sums, mix = groups[group]
+            mixed = (mix[...] * (1.0 / sums[...])).astype(BF)
             attended = dot(mixed, qkv[:, 2 * chans :]).astype(BF)
-            at_home = jnp.logical_and(same, slot == i)
-
-            @pl.when(at_home)
-            def _():
-                rbuf[slot] = attended
-
-            @pl.when(jnp.logical_not(at_home))
-            def _():
-                obuf[i] = attended
-                back(i).start()
+            start = 0
+            for c in (2 * group, 2 * group + 1):
+                first, count = CHUNKS[c]
+                for i in range(4):
+                    obuf[i, pl.ds(first, count)] = attended[start : start + count]
+                    start += count
+            for n in range(4):
+                i = lax.rem(slot + (2, 1, 3, 0)[n], 4)
+
+                @pl.when(jnp.logical_not(jnp.logical_and(same, slot == i)))
+                def _():
+                    back(group, i).start()
 
         own(0)
         project(0)
@@ -455,50 +476,50 @@
         project(1)
         beside(0)
         own(2)
-        project(2)
         beside(1)
         far(0)
+        project(2)
+        others(0)
+        attend(0, 0)
         own(3)
         project(3)
-        others(0)
-        attend(0, 0)
         beside(2)
+        far(1)
         attend(1, 0)
-        far(1)
-        attend(2, 0)
-        attend(3, 0)
         others(1)
+        beside(3)
         attend(0, 1)
-        beside(3)
+        far(2)
         attend(1, 1)
-        far(2)
-        attend(2, 1)
-        attend(3, 1)
         others(2)
         attend(0, 2)
         attend(1, 2)
         far(3)
-        attend(2, 2)
-        attend(3, 2)
         others(3)
-
-        @pl.loop(0, 4)
-        def _(n):
-            i = lax.rem(slot + 2 + jnp.where(n == 1, 3, jnp.where(n == 2, 1, n * 2)), 4)
-            attend(i, 3)
-            finish(i)
+        for group in range(2):
+            attend(group, 3)
+            finish(group)
+
+        @pl.when(same)
+        def _():
+            rbuf[slot] = obuf[slot]
 
         for c in sent:
             c.wait_send()
         for i in range(4):
-            pl.when(jnp.logical_not(jnp.logical_and(same, slot == i)))(back(i).wait_send)
+            @pl.when(jnp.logical_not(jnp.logical_and(same, slot == i)))
+            def _():
+                for group in range(2):
+                    back(group, i).wait_send()
 
     for j in range(3):
         @pl.when(2 * j + t != z)
         def _():
             for c in range(4):
                 home_copy(c, j).wait_send()
-            landed(rbuf.at[j], ret_recv.at[j])
+            for group in range(2):
+                part = pl.ds(CHUNKS[2 * group][0], CHUNKS[2 * group][1] + CHUNKS[2 * group + 1][1])
+                landed(rbuf.at[j, part], ret_recv.at[j, group])
 
         result = hid[j].astype(F32) + dot(rbuf[j], outw[...])
         for r in range(2):
@@ -506,6 +527,15 @@
 
     for cond, c in rims + prior:
         pl.when(cond)(c.wait_send)
+    for k in range(3):
+        for c in small_copies(k) + small_shares(k):
+            c.wait_send()
+    for core in range(2):
+        @pl.when(t == core)
+        def _():
+            for count, (sems, k, n) in sent[core]:
+                ref = wb.at[pl.ds(0, count)]
+                copy(ref, ref, sems.at[k, n], s_recv.at[0, 0], sib).wait_send()
 
 
 def on_device(
@@ -517,6 +547,7 @@
     smem = pl.BlockSpec(memory_space=pltpu.SMEM)
     hbm = pl.BlockSpec(memory_space=pltpu.HBM)
     dma = pltpu.SemaphoreType.DMA
+    queries = [4 * (CHUNKS[c][1] + CHUNKS[c + 1][1]) for c in (0, 2)]
     blocks = [pltpu.VMEM((XS, 2, 4, count, chans), BF) for _, count in CHUNKS]
     return pl.pallas_call(
         kernel,
@@ -534,15 +565,14 @@
             pltpu.VMEM((frames, pixels, chans), BF),
             pltpu.VMEM((frames, pixels, chans), BF),
             *blocks,
-            pltpu.VMEM((4, pixels, chans), BF),
-            pltpu.VMEM((4, pixels, 1), F32),
-            pltpu.VMEM((4, pixels, 1), F32),
-            pltpu.VMEM((4, pixels, chans), F32),
+            *[pltpu.VMEM((n, chans), BF) for n in queries],
+            *[pltpu.VMEM((n, 1), F32) for n in queries * 2],
+            *[pltpu.VMEM((n, chans), F32) for n in queries],
             pltpu.VMEM((4, pixels, chans), BF),
             pltpu.VMEM((3, pixels, chans), BF),
-            dma((4,)), dma((3, 4)), dma((3, 4)), dma((3, 2)), dma((3, 6)), dma((3, 8)),
-            dma((3, 4)), dma((3, 4)), dma((5,)), dma((5,)),
-            dma((4, 3)), dma((4, 4)), dma((4, 4)), dma((4, 4)), dma((4, 4)), dma((4, 4)), dma((4,)), dma((3,)),
+            dma((4,)), dma((3, 4)), dma((3, 4)), dma((3, 4)), dma((3, 3)), dma((3, 7)),
+            dma((3, 9)), dma((3, 9)), dma((3, 2)), dma((3, 2)), dma((5,)), dma((5,)),
+            dma((4, 3)), dma((4, 4)), dma((4, 4)), dma((4, 4)), dma((4, 4)), dma((4, 4)), dma((2, 4)), dma((3, 2)),
         ],
         compiler_params=pltpu.CompilerParams(
             collective_id=1, has_side_effects=True, vmem_limit_bytes=60 * 1024 * 1024

time: 111 us -> 107 us (0.964)
  Pallas kernels: 109 us -> 104 us
    pallas_call x1, Pallas kernels: 109 us -> 104 us  [on_device(): pl.pallas_call(kernel, out_shape=jax.ShapeDtypeStruct(features.shape, BF)...]
where the time goes in v4:
time: 107 us; the launch traced here: 106 us
  Pallas kernels  104 us (97%)
  local copies, waits for them, and re-layouts  1.85 us (2%)
    pallas_call x1, Pallas kernels, on_device(): pl.pallas_call(kernel, out_shape=jax.ShapeDtypeStruct(features.shape, BF)...  104 us

profile of v4, /device:TPU:1, one launch (start us, length us, event | category | flops | bytes accessed | tf_op | source)
XLA Modules:
  0.0 106.1 jit_solution(4171139462083762603)
XLA Ops:
  0.0 104.2 %shard_map.82 = bf16[1,3,2,104,384]{4,3,2,1,0:T(8,128)(2,1)} custom-call(bf16[1,3,2,104,384]{4,3,2,1,0:T(8,128)(2,1)} %feat.1, s32[1,3]{1,0:T(1,128)} %fidx.1, bf16[2592,384]{1,0:T(8,128)(2,1)} %w.1, bf16[96,1152]{1,0:T(8,128)(2,1)} %qkvw.1, bf16[96,384]{1,0:T(8,128)(2,1)} %ow.1, f32[384]{0:T(512)} %bias.1, f32[384]{0:T(512)} %norm_gain.1, f32[384]{0:T(512)} %attn_gain.1), custom_call_target="tpu_custom_call" | custom-call | flops 14210826240 | bytes 2949120 | tf_op jit(solution)/shard_map/pallas_call | solution.py:552
  104.2 1.8 %copy.10 = bf16[1,3,2,104,384]{4,3,2,1,0:T(8,128)(2,1)} copy(bf16[1,3,2,104,384]{4,3,2,1,0:T(8,128)(2,1)} %shard_map.82) | data formatting | bytes 958464

commit v5 on v4

--- a/solution.py
+++ b/solution.py
@@ -324,17 +324,21 @@
         spread_prior()
         on(2)
         mine[0].wait()
+        three_taps(y, 0)
         end(0)
-        three_taps(y, 0)
         rest(0)
+        three_taps(y, 1)
         end(1)
         rest(1)
+        shared(0)
+        three_taps(owner[0], 0)
         end(2)
         rest(2)
-        three_taps(y, 1)
-        for k in range(3):
-            shared(k)
-            six_taps(owner[k])
+        three_taps(owner[0], 1)
+        shared(1)
+        six_taps(owner[1])
+        shared(2)
+        six_taps(owner[2])
 
     for core in range(2):
         @pl.when(t == core)
@@ -476,25 +480,25 @@
         project(1)
         beside(0)
         own(2)
+        project(2)
         beside(1)
         far(0)
-        project(2)
+        own(3)
+        project(3)
         others(0)
         attend(0, 0)
-        own(3)
-        project(3)
         beside(2)
         far(1)
         attend(1, 0)
+        beside(3)
         others(1)
-        beside(3)
         attend(0, 1)
         far(2)
         attend(1, 1)
         others(2)
         attend(0, 2)
+        far(3)
         attend(1, 2)
-        far(3)
         others(3)
         for group in range(2):
             attend(group, 3)

time: 107 us -> 104 us (0.972)
  Pallas kernels: 104 us -> 102 us
    pallas_call x1, Pallas kernels: 104 us -> 102 us  [on_device(): pl.pallas_call(kernel, out_shape=jax.ShapeDtypeStruct(features.shape, BF)...]
where the time goes in v5:
time: 104 us; the launch traced here: 103 us
  Pallas kernels  102 us (98%)
  local copies, waits for them, and re-layouts  1.85 us (2%)
    pallas_call x1, Pallas kernels, on_device(): pl.pallas_call(kernel, out_shape=jax.ShapeDtypeStruct(features.shape, BF)...  102 us

profile of v5, /device:TPU:1, one launch (start us, length us, event | category | flops | bytes accessed | tf_op | source)
XLA Modules:
  0.0 103.5 jit_solution(6756272814255315975)
XLA Ops:
  0.0 101.6 %shard_map.82 = bf16[1,3,2,104,384]{4,3,2,1,0:T(8,128)(2,1)} custom-call(bf16[1,3,2,104,384]{4,3,2,1,0:T(8,128)(2,1)} %feat.1, s32[1,3]{1,0:T(1,128)} %fidx.1, bf16[2592,384]{1,0:T(8,128)(2,1)} %w.1, bf16[96,1152]{1,0:T(8,128)(2,1)} %qkvw.1, bf16[96,384]{1,0:T(8,128)(2,1)} %ow.1, f32[384]{0:T(512)} %bias.1, f32[384]{0:T(512)} %norm_gain.1, f32[384]{0:T(512)} %attn_gain.1), custom_call_target="tpu_custom_call" | custom-call | flops 14210826240 | bytes 2949120 | tf_op jit(solution)/shard_map/pallas_call | solution.py:556
  101.6 1.8 %copy.10 = bf16[1,3,2,104,384]{4,3,2,1,0:T(8,128)(2,1)} copy(bf16[1,3,2,104,384]{4,3,2,1,0:T(8,128)(2,1)} %shard_map.82) | data formatting | bytes 958464

commit v6 on v5

--- a/solution.py
+++ b/solution.py
@@ -322,9 +322,9 @@
         on(1)
         take_prior()
         spread_prior()
-        on(2)
         mine[0].wait()
         three_taps(y, 0)
+        on(2)
         end(0)
         rest(0)
         three_taps(y, 1)
@@ -347,6 +347,16 @@
 
     acc[...] += sum(dot(window(n), wb[rows(n * chans, chans)]) for n in (6, 13, 20))
 
+    kbs = (kb0, kb1, kb2, kb3)
+    groups = (q0, m0, l0, mix0), (q1, m1, l1, mix1)
+
+    def home_copy(c, j):
+        first, count = CHUNKS[c]
+        dst = kbs[c].at[x, parity, slot]
+        return copy(
+            nbuf.at[j, pl.ds(first, count)], dst, home_send.at[c, j], home_recv.at[c, slot], dev(parity, 2 * j + t, x)
+        )
+
     for f in range(3):
         both = []
         for r in range(2):
@@ -354,18 +364,9 @@
             both.append(featv[f, r].astype(F32) + part + bias[...])
         hid[f] = jnp.concatenate(both, axis=0).astype(BF)
         nbuf[f] = rms_scale(hid[f], attn_gain[...]).astype(BF)
-
-    kbs = (kb0, kb1, kb2, kb3)
-    groups = (q0, m0, l0, mix0), (q1, m1, l1, mix1)
-
-    def home_copy(c, j):
-        first, count = CHUNKS[c]
-        dst = kbs[c].at[x, parity, slot]
-        return copy(
-            nbuf.at[j, pl.ds(first, count)], dst, home_send.at[c, j], home_recv.at[c, slot], dev(parity, 2 * j + t, x)
-        )
-
-    for c in range(4):
+        pl.when(2 * f + t != z)(home_copy(0, f).start)
+
+    for c in range(1, 4):
         for j in range(3):
             pl.when(2 * j + t != z)(home_copy(c, j).start)
 

time: 104 us -> 103 us (level)
  no operation moved by 1% of the time
where the time goes in v6:
time: 103 us
  Pallas kernels  101 us (98%)
  local copies, waits for them, and re-layouts  1.85 us (2%)
    pallas_call x1, Pallas kernels, on_device(): pl.pallas_call(kernel, out_shape=jax.ShapeDtypeStruct(features.shape, BF)...  101 us

profile of v6, /device:TPU:1, one launch (start us, length us, event | category | flops | bytes accessed | tf_op | source)
XLA Modules:
  0.0 103.1 jit_solution(13978543558656136252)
XLA Ops:
  0.0 101.3 %shard_map.82 = bf16[1,3,2,104,384]{4,3,2,1,0:T(8,128)(2,1)} custom-call(bf16[1,3,2,104,384]{4,3,2,1,0:T(8,128)(2,1)} %feat.1, s32[1,3]{1,0:T(1,128)} %fidx.1, bf16[2592,384]{1,0:T(8,128)(2,1)} %w.1, bf16[96,1152]{1,0:T(8,128)(2,1)} %qkvw.1, bf16[96,384]{1,0:T(8,128)(2,1)} %ow.1, f32[384]{0:T(512)} %bias.1, f32[384]{0:T(512)} %norm_gain.1, f32[384]{0:T(512)} %attn_gain.1), custom_call_target="tpu_custom_call" | custom-call | flops 14210826240 | bytes 2949120 | tf_op jit(solution)/shard_map/pallas_call | solution.py:557
  101.3 1.8 %copy.10 = bf16[1,3,2,104,384]{4,3,2,1,0:T(8,128)(2,1)} copy(bf16[1,3,2,104,384]{4,3,2,1,0:T(8,128)(2,1)} %shard_map.82) | data formatting | bytes 958464
